TPU v7x, 256 devices: a whole 4x4x8 slice. The times are simulated.
256 devices in a mesh: chan: 32 (over z_lo, x, y), strip: 8 (over z_hi, core).
Axes of the slice: x: 4, y: 4, z: 8 (z_hi: 4, z_lo: 2; z = z_hi * 2 + z_lo), core: 2. Of those that a mesh axis runs over, the one named last changes fastest.
Arguments:
- voltages: bfloat16 [2048, 292864], P(('strip', 'chan')), may hold values from -6 to 6
- taps: float32 [16, 2048], replicated, may hold values from -1.5 to 1.5
Outputs:
- visibilities: bfloat16 [64, 4096, 4096], P('chan', 'strip')
All inputs are finite; a program needn't handle non-finite values.
Results may differ from a plain program's by a relative error of at most 0.0076.
Values may be sent and summed in bfloat16 or wider, within the bound.
No kernel may reach another device: no remote copies, remote signals or barrier semaphores. Data moves between devices by JAX's collectives and lax.ppermute only.
A program may use at most 128 MiB of HBM per device.

v0:
```python
import math

import jax
import jax.numpy as jnp
from jax import lax
from jax.sharding import PartitionSpec as P

FRAME_LEN = 2048
CHANNELS = 64
SLAB0 = 384
FRAMES = 128


def slab_table(length, channels, first):
    sample = jnp.arange(length, dtype=jnp.int32)[:, None]
    channel_ids = (first + jnp.arange(channels, dtype=jnp.int32))[None, :]
    phase_index = sample * channel_ids % length
    angles = phase_index.astype(jnp.float32) * (2.0 * math.pi / length)
    norm_scale = (2.0 / length) ** 0.5
    return jnp.concatenate(
        [jnp.cos(angles) * norm_scale, -jnp.sin(angles) * norm_scale], axis=1
    ).astype(jnp.bfloat16)


def channelize(signal, taps, dft_table, frame_lo, frame_count):
    inputs_here = signal.shape[0]
    length = taps.shape[1]
    framed = signal.reshape(inputs_here, -1, length)
    filtered = jnp.zeros((inputs_here, frame_count, length), jnp.float32)
    for tap_index in range(taps.shape[0]):
        window = lax.slice_in_dim(
            framed, frame_lo + tap_index, frame_lo + tap_index + frame_count, axis=1
        )
        filtered = filtered + taps[tap_index] * window.astype(jnp.float32)
    flat = filtered.astype(jnp.bfloat16).reshape(inputs_here * frame_count, length)
    spectra = jnp.dot(flat, dft_table, preferred_element_type=jnp.float32).astype(jnp.bfloat16)
    channels = dft_table.shape[1] // 2
    spectra = spectra.reshape(inputs_here, frame_count, 2, channels)
    return jnp.transpose(spectra, (3, 0, 2, 1)).reshape(channels, 2 * inputs_here, frame_count)


def shards(voltages, taps):
    dft_table = slab_table(FRAME_LEN, CHANNELS, SLAB0)
    inputs_here = voltages.shape[0]
    chan_count = lax.axis_size("chan")
    strip_count = lax.axis_size("strip")
    spectra = channelize(voltages, taps, dft_table, 0, FRAMES)
    gathered = lax.all_gather(spectra, "strip", axis=1, tiled=True)
    shaped = gathered.reshape(spectra.shape[0], strip_count, 1, 2 * inputs_here, FRAMES)
    turned = lax.all_to_all(shaped, "chan", split_axis=0, concat_axis=2, tiled=True)
    all_rows = turned.reshape(turned.shape[0], -1, FRAMES)
    row_count = chan_count * 2 * inputs_here
    own_rows = lax.dynamic_slice_in_dim(all_rows, lax.axis_index("strip") * row_count, row_count, 1)
    summed = jnp.einsum("crf,cqf->crq", own_rows, all_rows, preferred_element_type=jnp.float32)
    return (summed * (1.0 / FRAMES)).astype(jnp.bfloat16)


def solution(mesh):
    placed = (P(("strip", "chan"), None), P())
    return jax.shard_map(
        shards, mesh=mesh, in_specs=placed, out_specs=P("chan", "strip", None), check_vma=False
    )
```

profile of v0, /device:TPU:33, one launch (start us, length us, event | category | flops | bytes accessed | tf_op | source)
XLA Modules:
  0.0 140.2 jit_solution(2551196204734614318)
XLA Ops:
  6.5 0.0 all-gather.2.cloned.1.call-start
  6.5 1.6 %fusion.12 = (f32[1,2048]{1,0:T(1,128)S(1)}, f32[1,2048]{1,0:T(1,128)S(1)}, f32[1,2048]{1,0:T(1,128)S(1)}, f32[1,2048]{1,0:T(1,128)S(1)}, f32[1,2048]{1,0:T(1,12...) fusion(f32[16,2048]{1,0:T(8,128)} %param.3), kind=kLoop, calls=%fused_computation.21 | loop fusion | bytes 262144 | tf_op jit(solution)/shard_map/slice | solution.py:34
  8.1 2.5 %multiply_convert_fusion.2 = (bf16[2048,64]{0,1:T(8,128)(2,1)S(1)}, bf16[2048,64]{0,1:T(8,128)(2,1)S(1)}) fusion(s32[64]{0:T(128)S(1)} %iota_add_fusion), kind=kLoop, calls=%fused_computation.13 | loop fusion | flops 2490368 | bytes 524544 | tf_op jit(solution)/shard_map/convert
  10.6 33.6 %add_convert_fusion = bf16[8,128,2048]{2,0,1:T(8,128)(2,1)S(1)} fusion(bf16[8,143,2048]{2,0,1:T(8,128)(2,1)} %bitcast.33, f32[2048]{0:T(1024)S(1)} %bitcast.55, f32[2048]{0:T(1024)S(1)} %bitcast.56, f32[2048]{0:T(1024)S(1)} %bitcast.42, f32[2048]{0:T(1024)S(1)} %bitcast.43, f32[2048]{0:T(1024)S(1)} %bitcast.44, f32[2048]{0:T(1024)S(1)} %bitcast.45, ...), kind=kLoop, calls=%fused_computation.1 | loop fusion | flops 100663296 | bytes 71434240 | tf_op jit(solution)/shard_map/convert_element_type | solution.py:35
  44.2 2.3 %copy.17 = bf16[8,128,2048]{2,1,0:T(8,128)(2,1)S(1)} copy(bf16[8,128,2048]{2,0,1:T(8,128)(2,1)S(1)} %add_convert_fusion) | data formatting | bytes 8388608 | tf_op jit(solution)/shard_map/convert_element_type | solution.py:35
  46.5 1.3 convolution_convert_fusion
  47.8 0.1 copy.18
  48.0 0.8 copy.19
  48.8 0.0 all-gather.2.cloned.1.call-update
  48.8 38.6 %all-gather.2.cloned.1.call-done = bf16[64,128,128]{2,0,1:T(8,128)(2,1)} async-done(((bf16[64,16,128]{2,0,1:T(8,128)(2,1)}), bf16[64,128,128]{2,0,1:T(8,128)(2,1)}) %all-gather.2.cloned.1.call-update) | async-done | bytes 2097168 | tf_op jit(solution)/shard_map/all_gather | solution.py:48
  87.4 4.3 %copy.20 = bf16[64,8,1,16,128]{4,3,1,2,0:T(8,128)(2,1)} copy(bf16[64,8,1,16,128]{4,0,3,1,2:T(8,128)(2,1)} %bitcast.37) | data formatting | bytes 4194304 | tf_op jit(solution)/shard_map/reshape | solution.py:49
  91.7 7.9 %all-to-all-start = ((bf16[64,8,1,16,128]{4,3,1,2,0:T(8,128)(2,1)}), bf16[64,8,1,16,128]{4,3,1,2,0:T(8,128)(2,1)S(1)}, u32[]{:S(2)}, u32[]{:S(2)}) async-start(bf16[64,8,1,16,128]{4,3,1,2,0:T(8,128)(2,1)} %copy.20), calls=%async_computation | async-start | bytes 4194304 | tf_op jit(solution)/shard_map/all_to_all | solution.py:50
  99.5 27.6 %all-to-all-done = bf16[64,8,1,16,128]{4,3,1,2,0:T(8,128)(2,1)S(1)} async-done(((bf16[64,8,1,16,128]{4,3,1,2,0:T(8,128)(2,1)}), bf16[64,8,1,16,128]{4,3,1,2,0:T(8,128)(2,1)S(1)}, u32[]{:S(2)}, u32[]{:S(2)}) %all-to-all-start) | async-done | bytes 2097184 | tf_op jit(solution)/shard_map/all_to_all | solution.py:50
  127.1 0.5 copy.21
  127.6 5.8 %multiply_convert_fusion = bf16[2,512,4096]{2,1,0:T(8,128)(2,1)} fusion(bf16[2,4096,128]{2,1,0:T(8,128)(2,1)S(1)} %bitcast.35, s32[]{:T(128)S(6)} %select_n.13), kind=kOutput, calls=%fused_computation | convolution fusion | flops 1082130432 | bytes 10747908 | tf_op jit(solution)/shard_map/crf,cqf->crq/dot_general | solution.py:54
  (2 shorter events, 0.0 us)
Async XLA Ops:
  6.5 80.9 %all-gather.2.cloned.1.call-start = ((), (), s32[]{:S(2)}) async-start(), calls=%async_computation.1 | async-start | bytes 2359296 | tf_op jit(solution)/shard_map/all_gather | solution.py:48
  91.7 35.5 %all-to-all-start = ((bf16[64,8,1,16,128]{4,3,1,2,0:T(8,128)(2,1)}), bf16[64,8,1,16,128]{4,3,1,2,0:T(8,128)(2,1)S(1)}, u32[]{:S(2)}, u32[]{:S(2)}) async-start(bf16[64,8,1,16,128]{4,3,1,2,0:T(8,128)(2,1)} %copy.20), calls=%async_computation | async-start | bytes 4194304 | tf_op jit(solution)/shard_map/all_to_all | solution.py:50
Sparse Core Ops, SparseCore 0:
  48.9 38.4 all-gather.1
where the time goes:
time: 142 us; the launch traced here: 140 us
  waiting for transfers between devices  66.2 us (47%)
  other arithmetic  36 us (25%)
  between operations  13.5 us (10%)
  local copies, waits for them, and re-layouts  9.59 us (7%)
  starting transfers between devices  7.87 us (6%)
  matrix products  7.04 us (5%)
    all_gather x1, waiting for transfers between devices, shards(): gathered = lax.all_gather(spectra, 'strip', axis=1, tiled=True)  38.6 us
    convert_element_type x1, other arithmetic, channelize(): filtered.astype(jnp.bfloat16).reshape(inputs_here * frame_count, length)  33.6 us
    all_to_all x1, waiting for transfers between devices, shards(): lax.all_to_all(shaped, 'chan', split_axis=0, concat_axis=2, tiled=True)  27.6 us
    all_to_all x1, starting transfers between devices, shards(): lax.all_to_all(shaped, 'chan', split_axis=0, concat_axis=2, tiled=True)  7.87 us
    dot_general x1, matrix products, shards(): jnp.einsum('crf,cqf->crq', own_rows, all_rows, preferred_element_type=jnp...  5.75 us
    reshape x1, local copies, waits for them, and re-layouts, shards(): gathered.reshape(spectra.shape[0], strip_count, 1, 2 * inputs_here, FRAMES)  4.26 us
  transfers between devices with their start and end apart: 2, of which 2 were waited for; matrix products, arithmetic and copies ran while one was open for 0% of the time, Pallas kernels for 0%

commit v1 on v0

v1 whole, which is shorter than its diff:
```python
import math

import jax
import jax.numpy as jnp
import ml_dtypes
import numpy as np
from jax import lax
from jax.experimental import pallas as pl
from jax.experimental.pallas import tpu as pltpu
from jax.sharding import Mesh
from jax.sharding import PartitionSpec as P

FRAME_LEN = 2048
CHANNELS = 64
SLAB0 = 384
FRAMES = 128
TAPS = 16
INPUTS_HERE = 8
LANES = 128
CHUNK = 128
PEERS = 32
OWN = CHANNELS // PEERS
ROWS = 2 * INPUTS_HERE
STRIP_ROWS = PEERS * ROWS
STRIPS = 8
VMEM_LIMIT = 48 * 2**20


def slab_table():
    sample = np.arange(FRAME_LEN, dtype=np.int64)[:, None]
    channel_ids = SLAB0 + np.arange(CHANNELS, dtype=np.int64)[None, :]
    phase_index = sample * channel_ids % FRAME_LEN
    angles = phase_index.astype(np.float32) * np.float32(2.0 * math.pi / FRAME_LEN)
    norm_scale = np.float32((2.0 / FRAME_LEN) ** 0.5)
    return np.concatenate(
        [np.cos(angles) * norm_scale, -np.sin(angles) * norm_scale], axis=1
    ).astype(ml_dtypes.bfloat16)


def channelize_kernel(
    volt_hbm, taps_hbm, table_hbm, out_ref, volt, taps, table, filtered, product, turned, sems
):
    parts = FRAMES // CHUNK
    lands = []
    low = 0
    for part in range(parts):
        high = (part + 1) * CHUNK + TAPS - 1
        span = pl.ds(low * FRAME_LEN, (high - low) * FRAME_LEN)
        lands.append(
            pltpu.make_async_copy(volt_hbm.at[:, span], volt.at[:, span], sems.at[part])
        )
        low = high
    taps_copy = pltpu.make_async_copy(taps_hbm, taps, sems.at[parts])
    table_copy = pltpu.make_async_copy(table_hbm, table, sems.at[parts + 1])
    taps_copy.start()
    for land in lands:
        land.start()
    table_copy.start()
    taps_copy.wait()
    for part in range(parts):
        first = part * CHUNK
        lands[part].wait()

        def column(tile, carry):
            lane = pl.multiple_of(tile * LANES, LANES)
            weights = [
                jnp.broadcast_to(taps[pl.ds(t, 1), pl.ds(lane, LANES)], (INPUTS_HERE, LANES))
                for t in range(TAPS)
            ]
            sums = {}
            before = None
            for g in range(CHUNK + TAPS - 1):
                start = pl.multiple_of((first + g) * FRAME_LEN + lane, LANES)
                sample = volt[:, pl.ds(start, LANES)].astype(jnp.float32)
                for t in range(TAPS):
                    f = g - t
                    if 0 <= f < CHUNK:
                        term = weights[t] * sample
                        sums[f] = sums[f] + term if f in sums else term
                f = g - (TAPS - 1)
                if f >= 0 and f % 2 == 0:
                    before = sums.pop(f)
                elif f >= 0:
                    pair = jnp.concatenate([before, sums.pop(f)], axis=0)
                    rows = pl.ds((first + f - 1) * INPUTS_HERE, 2 * INPUTS_HERE)
                    filtered[rows, pl.ds(lane, LANES)] = pair.astype(jnp.bfloat16)
            return carry

        lax.fori_loop(0, FRAME_LEN // LANES, column, 0)
    table_copy.wait()
    product[...] = jnp.dot(filtered[...], table[...], preferred_element_type=jnp.float32)
    for i in range(INPUTS_HERE):
        turned[i * LANES : (i + 1) * LANES, :] = product[
            pl.ds(i, FRAMES, stride=INPUTS_HERE), :
        ].T

    def channel(c, carry):
        out_ref[c] = turned[pl.ds(c, ROWS, stride=CHANNELS), :].astype(jnp.bfloat16)
        return carry

    lax.fori_loop(0, CHANNELS, channel, 0, unroll=16)


def channelize(volt, taps, table):
    parts = FRAMES // CHUNK
    return pl.pallas_call(
        channelize_kernel,
        out_shape=jax.ShapeDtypeStruct((CHANNELS, ROWS, FRAMES), jnp.bfloat16),
        in_specs=[pl.BlockSpec(memory_space=pl.ANY)] * 3,
        out_specs=pl.BlockSpec(memory_space=pltpu.VMEM),
        scratch_shapes=[
            pltpu.VMEM(volt.shape, jnp.bfloat16),
            pltpu.VMEM((TAPS, FRAME_LEN), jnp.float32),
            pltpu.VMEM((FRAME_LEN, 2 * CHANNELS), jnp.bfloat16),
            pltpu.VMEM((FRAMES * INPUTS_HERE, FRAME_LEN), jnp.bfloat16),
            pltpu.VMEM((FRAMES * INPUTS_HERE, 2 * CHANNELS), jnp.float32),
            pltpu.VMEM((FRAMES * INPUTS_HERE, FRAMES), jnp.float32),
            pltpu.SemaphoreType.DMA((parts + 2,)),
        ],
        compiler_params=pltpu.CompilerParams(vmem_limit_bytes=VMEM_LIMIT),
    )(volt, taps, table)


def correlate_kernel(*refs):
    blocks, out_hbm, stage, sems = refs[:STRIPS], refs[STRIPS], refs[STRIPS + 1], refs[STRIPS + 2]
    z_hi = lax.axis_index("z_hi")
    core = lax.axis_index("core")
    writes = [None, None]
    step = 0
    for ch in range(OWN):
        left = blocks[0][:, ch].reshape(STRIP_ROWS, FRAMES)
        for b in range(STRIPS):
            slot = step % 2
            strip = lax.rem(z_hi + STRIPS // 2 - b // 2, STRIPS // 2) * 2 + lax.rem(core + b % 2, 2)
            right = blocks[b][:, ch].reshape(STRIP_ROWS, FRAMES)
            got = lax.dot_general(
                left, right, (((1,), (1,)), ((), ())), preferred_element_type=jnp.float32
            )
            if writes[slot] is not None:
                writes[slot].wait()
            stage[slot] = (got * (1.0 / FRAMES)).astype(jnp.bfloat16)
            span = pl.ds(pl.multiple_of(strip * STRIP_ROWS, STRIP_ROWS), STRIP_ROWS)
            writes[slot] = pltpu.make_async_copy(
                stage.at[slot], out_hbm.at[ch, :, span], sems.at[slot]
            )
            writes[slot].start()
            step += 1
    for write in writes:
        write.wait()


def correlate(blocks):
    return pl.pallas_call(
        correlate_kernel,
        out_shape=jax.ShapeDtypeStruct((OWN, STRIP_ROWS, STRIPS * STRIP_ROWS), jnp.bfloat16),
        in_specs=[pl.BlockSpec(memory_space=pltpu.VMEM)] * STRIPS,
        out_specs=pl.BlockSpec(memory_space=pl.ANY),
        scratch_shapes=[
            pltpu.VMEM((2, STRIP_ROWS, STRIP_ROWS), jnp.bfloat16),
            pltpu.SemaphoreType.DMA((2,)),
        ],
        compiler_params=pltpu.CompilerParams(vmem_limit_bytes=VMEM_LIMIT),
    )(*blocks)


def shift(block, by):
    return lax.ppermute(block, "z_hi", [(i, (i + by) % 4) for i in range(4)])


def swap(block):
    return lax.ppermute(block, "core", [(0, 1), (1, 0)])


def shards(volt, taps):
    spectra = channelize(volt, taps, jnp.asarray(slab_table()))
    own = lax.all_to_all(spectra, ("z_lo", "x", "y"), split_axis=0, concat_axis=0, tiled=True)
    own = own.reshape(PEERS, OWN, ROWS, FRAMES)
    blocks = []
    for by in range(4):
        block = shift(own, by) if by else own
        blocks += [block, swap(block)]
    return correlate(blocks)


def solution(mesh):
    fine = Mesh(mesh.devices.reshape(2, 4, 4, 4, 2), ("z_lo", "x", "y", "z_hi", "core"))
    inputs = ("z_hi", "core", "z_lo", "x", "y")
    return jax.shard_map(
        shards,
        mesh=fine,
        in_specs=(P(inputs, None), P()),
        out_specs=P(("z_lo", "x", "y"), ("z_hi", "core"), None),
        check_vma=False,
    )
```

time: 142 us -> 72.6 us (0.51); the launches traced: 140 us -> 72.4 us
  waiting for transfers between devices: 66.2 us -> 5.76 us
  other arithmetic: 36 us -> 0 us
  Pallas kernels: 0 us -> 20.7 us
  starting transfers between devices: 7.87 us -> 26.4 us
  blocking collectives: 0 us -> 15.3 us
  between operations: 13.5 us -> 0.02 us
  matrix products: 7.04 us -> 0 us
  local copies, waits for them, and re-layouts: 9.59 us -> 4.27 us
    all_gather x1 -> x0, waiting for transfers between devices: 38.6 us -> none  [shards(): gathered = lax.all_gather(spectra, 'strip', axis=1, tiled=True)]
    convert_element_type x1 -> x0, other arithmetic: 33.6 us -> none  [channelize(): filtered.astype(jnp.bfloat16).reshape(inputs_here * frame_count, length)]
    all_to_all x1 -> x0, waiting for transfers between devices: 27.6 us -> none  [shards(): lax.all_to_all(shaped, 'chan', split_axis=0, concat_axis=2, tiled=True)]
    ppermute x0 -> x7, starting transfers between devices: none -> 26.4 us  [the longest x4 18 us: swap(): return lax.ppermute(block, 'core', [(0, 1), (1, 0)])]
    pallas_call x0 -> x2, Pallas kernels: none -> 20.7 us  [the longest x1 11.7 us: channelize(): pl.pallas_call(channelize_kernel, out_shape=jax.ShapeDtypeStruct((CHANNEL...]
    all_to_all x0 -> x1, blocking collectives: none -> 15.3 us  [shards(): lax.all_to_all(spectra, ('z_lo', 'x', 'y'), split_axis=0, concat_axis=0,...]
    all_to_all x1 -> x0, starting transfers between devices: 7.87 us -> none  [shards(): lax.all_to_all(shaped, 'chan', split_axis=0, concat_axis=2, tiled=True)]
    dot_general x2 -> x0, matrix products: 7.04 us -> none  [the longest x1 5.75 us: shards(): jnp.einsum('crf,cqf->crq', own_rows, all_rows, preferred_element_type=jnp...]
  transfers between devices with their start and end apart: 2 -> 7, of which waited for: 2 -> 4; matrix products, arithmetic and copies ran while one was open for 0% -> 0% of each run, Pallas kernels for 0% -> 0%
where the time goes in v1:
time: 72.6 us; the launch traced here: 72.4 us
  starting transfers between devices  26.4 us (36%)
  Pallas kernels  20.7 us (29%)
  blocking collectives  15.3 us (21%)
  waiting for transfers between devices  5.76 us (8%)
  local copies, waits for them, and re-layouts  4.27 us (6%)
    ppermute x4, starting transfers between devices, swap(): return lax.ppermute(block, 'core', [(0, 1), (1, 0)])  18 us
    all_to_all x1, blocking collectives, shards(): lax.all_to_all(spectra, ('z_lo', 'x', 'y'), split_axis=0, concat_axis=0,...  15.3 us
    pallas_call x1, Pallas kernels, channelize(): pl.pallas_call(channelize_kernel, out_shape=jax.ShapeDtypeStruct((CHANNEL...  11.7 us
    pallas_call x1, Pallas kernels, correlate(): pl.pallas_call(correlate_kernel, out_shape=jax.ShapeDtypeStruct((OWN, STR...  9.01 us
    ppermute x3, starting transfers between devices, shift(): return lax.ppermute(block, 'z_hi', [(i, (i + by) % 4) for i in range(4)])  8.38 us
    ppermute x3, waiting for transfers between devices, shift(): return lax.ppermute(block, 'z_hi', [(i, (i + by) % 4) for i in range(4)])  4.6 us
    unnamed x6, local copies, waits for them, and re-layouts  4.27 us
  transfers between devices with their start and end apart: 7, of which 4 were waited for; matrix products, arithmetic and copies ran while one was open for 0% of the time, Pallas kernels for 0%

profile of v1, /device:TPU:33, one launch (start us, length us, event | category | flops | bytes accessed | tf_op | source)
XLA Modules:
  0.0 72.4 jit_solution(7771732093591510333)
XLA Ops:
  0.0 0.0 copy-start
  0.0 2.3 %copy-done = bf16[8,292864]{1,0:T(8,128)(2,1)S(1)} copy-done((bf16[8,292864]{1,0:T(8,128)(2,1)S(1)}, bf16[8,292864]{1,0:T(8,128)(2,1)}, u32[]{:S(2)}) %copy-start) | copy-done | bytes 4685848
  2.3 0.0 copy-start.1
  2.3 1.0 %copy-done.1 = bf16[2048,128]{1,0:T(8,128)(2,1)S(1)} copy-done((bf16[2048,128]{1,0:T(8,128)(2,1)S(1)}, bf16[2048,128]{1,0:T(8,128)(2,1)}, u32[]{:S(2)}) %copy-start.1) | copy-done | bytes 524312
  3.4 0.0 copy-start.2
  3.4 0.9 %copy-done.2 = f32[16,2048]{1,0:T(8,128)S(1)} copy-done((f32[16,2048]{1,0:T(8,128)S(1)}, f32[16,2048]{1,0:T(8,128)}, u32[]{:S(2)}) %copy-start.2) | copy-done | bytes 131096
  4.3 11.7 %shard_map.37 = bf16[64,16,128]{2,1,0:T(8,128)(2,1)S(1)} custom-call(bf16[8,292864]{1,0:T(8,128)(2,1)S(1)} %copy-done, f32[16,2048]{1,0:T(8,128)S(1)} %copy-done.2, bf16[2048,128]{1,0:T(8,128)(2,1)S(1)} %copy-done.1), custom_call_target="tpu_custom_call" | custom-call | tf_op jit(solution)/shard_map/pallas_call | solution.py:106
  16.0 15.3 %all_to_all.5 = bf16[64,16,128]{2,1,0:T(8,128)(2,1)S(1)} all-to-all(bf16[64,16,128]{2,1,0:T(8,128)(2,1)S(1)} %shard_map.37), channel_id=1, replica_groups=mesh['z_lo'=2,'x'=4,'y'=4,'z_hi'=4,'core'=2] {'z_lo','x','y'}, dimensions={0} | all-to-all | bytes 524288 | tf_op jit(solution)/shard_map/all_to_all | solution.py:176
  31.3 5.1 %collective-permute-start.5 = (bf16[32,2,16,128]{3,2,1,0:T(8,128)(2,1)S(1)}, bf16[32,2,16,128]{3,2,1,0:T(8,128)(2,1)S(1)}, u32[]{:S(2)}, u32[]{:S(2)}) collective-permute-start(bf16[32,2,16,128]{3,2,1,0:T(8,128)(2,1)S(1)} %bitcast.1), channel_id=1, source_target_pairs={{0,6},{2,0},{4,2},{6,4},{1,7},{3,1},{5,3},{7,5},{8,14},{10,8},{12,... | collective-permute-start | bytes 786440 | tf_op jit(solution)/shard_map/ppermute | solution.py:167
  36.4 1.2 %collective-permute-start.3 = (bf16[32,2,16,128]{3,2,1,0:T(8,128)(2,1)S(1)}, bf16[32,2,16,128]{3,2,1,0:T(8,128)(2,1)S(1)}, u32[]{:S(2)}, u32[]{:S(2)}) collective-permute-start(bf16[32,2,16,128]{3,2,1,0:T(8,128)(2,1)S(1)} %bitcast.2), channel_id=1, source_target_pairs={{0,4},{2,6},{4,0},{6,2},{1,5},{3,7},{5,1},{7,3},{8,12},{10,14},{12... | collective-permute-start | bytes 786440 | tf_op jit(solution)/shard_map/ppermute | solution.py:167
  37.6 2.1 %collective-permute-start.1 = (bf16[32,2,16,128]{3,2,1,0:T(8,128)(2,1)S(1)}, bf16[32,2,16,128]{3,2,1,0:T(8,128)(2,1)S(1)}, u32[]{:S(2)}, u32[]{:S(2)}) collective-permute-start(bf16[32,2,16,128]{3,2,1,0:T(8,128)(2,1)S(1)} %bitcast.3), channel_id=1, source_target_pairs={{0,2},{2,4},{4,6},{6,0},{1,3},{3,5},{5,7},{7,1},{8,10},{10,12},{12... | collective-permute-start | bytes 786440 | tf_op jit(solution)/shard_map/ppermute | solution.py:167
  39.7 2.6 %collective-permute-start = (bf16[32,2,16,128]{3,2,1,0:T(8,128)(2,1)S(1)}, bf16[32,2,16,128]{3,2,1,0:T(8,128)(2,1)S(1)}, u32[]{:S(2)}, u32[]{:S(2)}) collective-permute-start(bf16[32,2,16,128]{3,2,1,0:T(8,128)(2,1)S(1)} %bitcast.4), channel_id=1, source_target_pairs={{0,1},{1,0},{2,3},{3,2},{4,5},{5,4},{6,7},{7,6},{8,9},{9,8},{10,11... | collective-permute-start | bytes 786440 | tf_op jit(solution)/shard_map/ppermute | solution.py:171
  42.3 0.6 collective-permute-done.5.refs_6_
  43.0 12.6 %collective-permute-start.6 = (bf16[32,2,16,128]{3,2,1,0:T(8,128)(2,1)S(1)}, bf16[32,2,16,128]{3,2,1,0:T(8,128)(2,1)S(1)}, u32[]{:S(2)}, u32[]{:S(2)}) collective-permute-start(bf16[32,2,16,128]{3,2,1,0:T(8,128)(2,1)S(1)} %collective-permute-done.5.refs_6_), channel_id=1, source_target_pairs={{0,1},{1,0},{2,3},{3,2},{4,5},{5,4},{6,7},{7,6},{8,9},{9,8},{10,11... | collective-permute-start | bytes 786440 | tf_op jit(solution)/shard_map/ppermute | solution.py:171
  55.6 4.0 %collective-permute-done.3.refs_4_ = bf16[32,2,16,128]{3,2,1,0:T(8,128)(2,1)S(1)} collective-permute-done((bf16[32,2,16,128]{3,2,1,0:T(8,128)(2,1)S(1)}, bf16[32,2,16,128]{3,2,1,0:T(8,128)(2,1)S(1)}, u32[]{:S(2)}, u32[]{:S(2)}) %collective-permute-start.3) | collective-permute-done | bytes 262176 | tf_op jit(solution)/shard_map/ppermute | solution.py:167
  59.5 2.2 %collective-permute-start.4 = (bf16[32,2,16,128]{3,2,1,0:T(8,128)(2,1)S(1)}, bf16[32,2,16,128]{3,2,1,0:T(8,128)(2,1)S(1)}, u32[]{:S(2)}, u32[]{:S(2)}) collective-permute-start(bf16[32,2,16,128]{3,2,1,0:T(8,128)(2,1)S(1)} %collective-permute-done.3.refs_4_), channel_id=1, source_target_pairs={{0,1},{1,0},{2,3},{3,2},{4,5},{5,4},{6,7},{7,6},{8,9},{9,8},{10,11... | collective-permute-start | bytes 786440 | tf_op jit(solution)/shard_map/ppermute | solution.py:171
  61.7 0.0 collective-permute-done.1.refs_2_
  61.7 0.5 collective-permute-start.2
  62.3 0.0 collective-permute-done.refs_1_
  62.3 0.0 collective-permute-done.6.refs_7_
  62.3 0.6 collective-permute-done.4.refs_5_
  62.9 0.5 collective-permute-done.2.refs_3_
  63.4 9.0 %shard_map.38 = bf16[2,512,4096]{2,1,0:T(8,128)(2,1)} custom-call(bf16[32,2,16,128]{3,2,1,0:T(8,128)(2,1)S(1)} %bitcast.5, bf16[32,2,16,128]{3,2,1,0:T(8,128)(2,1)S(1)} %collective-permute-done.refs_1_, bf16[32,2,16,128]{3,2,1,0:T(8,128)(2,1)S(1)} %collective-permute-done.1.refs_2_, bf16[32,2,16,128]{3,2,1,0:T(8,128)(2,1)S(1)} %collective-permute-done.2.refs_3_, ...), custom_call_target="tpu_custom_call" | custom-call | tf_op jit(solution)/shard_map/pallas_call | solution.py:153
Async XLA Ops:
  0.0 2.3 %copy-start = (bf16[8,292864]{1,0:T(8,128)(2,1)S(1)}, bf16[8,292864]{1,0:T(8,128)(2,1)}, u32[]{:S(2)}) copy-start(bf16[8,292864]{1,0:T(8,128)(2,1)} %volt_hbm.1) | copy-start | bytes 14057476
  2.3 1.0 %copy-start.1 = (bf16[2048,128]{1,0:T(8,128)(2,1)S(1)}, bf16[2048,128]{1,0:T(8,128)(2,1)}, u32[]{:S(2)}) copy-start(bf16[2048,128]{1,0:T(8,128)(2,1)} %constant.2.clone.table_hbm) | copy-start | bytes 1572868
  3.4 0.9 %copy-start.2 = (f32[16,2048]{1,0:T(8,128)S(1)}, f32[16,2048]{1,0:T(8,128)}, u32[]{:S(2)}) copy-start(f32[16,2048]{1,0:T(8,128)} %taps_hbm.1) | copy-start | bytes 393220
  31.3 11.7 %collective-permute-start.5 = (bf16[32,2,16,128]{3,2,1,0:T(8,128)(2,1)S(1)}, bf16[32,2,16,128]{3,2,1,0:T(8,128)(2,1)S(1)}, u32[]{:S(2)}, u32[]{:S(2)}) collective-permute-start(bf16[32,2,16,128]{3,2,1,0:T(8,128)(2,1)S(1)} %bitcast.1), channel_id=1, source_target_pairs={{0,6},{2,0},{4,2},{6,4},{1,7},{3,1},{5,3},{7,5},{8,14},{10,8},{12,... | collective-permute-start | bytes 786440 | tf_op jit(solution)/shard_map/ppermute | solution.py:167
  36.4 23.1 %collective-permute-start.3 = (bf16[32,2,16,128]{3,2,1,0:T(8,128)(2,1)S(1)}, bf16[32,2,16,128]{3,2,1,0:T(8,128)(2,1)S(1)}, u32[]{:S(2)}, u32[]{:S(2)}) collective-permute-start(bf16[32,2,16,128]{3,2,1,0:T(8,128)(2,1)S(1)} %bitcast.2), channel_id=1, source_target_pairs={{0,4},{2,6},{4,0},{6,2},{1,5},{3,7},{5,1},{7,3},{8,12},{10,14},{12... | collective-permute-start | bytes 786440 | tf_op jit(solution)/shard_map/ppermute | solution.py:167
  37.6 24.2 %collective-permute-start.1 = (bf16[32,2,16,128]{3,2,1,0:T(8,128)(2,1)S(1)}, bf16[32,2,16,128]{3,2,1,0:T(8,128)(2,1)S(1)}, u32[]{:S(2)}, u32[]{:S(2)}) collective-permute-start(bf16[32,2,16,128]{3,2,1,0:T(8,128)(2,1)S(1)} %bitcast.3), channel_id=1, source_target_pairs={{0,2},{2,4},{4,6},{6,0},{1,3},{3,5},{5,7},{7,1},{8,10},{10,12},{12... | collective-permute-start | bytes 786440 | tf_op jit(solution)/shard_map/ppermute | solution.py:167
  39.7 22.6 %collective-permute-start = (bf16[32,2,16,128]{3,2,1,0:T(8,128)(2,1)S(1)}, bf16[32,2,16,128]{3,2,1,0:T(8,128)(2,1)S(1)}, u32[]{:S(2)}, u32[]{:S(2)}) collective-permute-start(bf16[32,2,16,128]{3,2,1,0:T(8,128)(2,1)S(1)} %bitcast.4), channel_id=1, source_target_pairs={{0,1},{1,0},{2,3},{3,2},{4,5},{5,4},{6,7},{7,6},{8,9},{9,8},{10,11... | collective-permute-start | bytes 786440 | tf_op jit(solution)/shard_map/ppermute | solution.py:171
  43.0 19.3 %collective-permute-start.6 = (bf16[32,2,16,128]{3,2,1,0:T(8,128)(2,1)S(1)}, bf16[32,2,16,128]{3,2,1,0:T(8,128)(2,1)S(1)}, u32[]{:S(2)}, u32[]{:S(2)}) collective-permute-start(bf16[32,2,16,128]{3,2,1,0:T(8,128)(2,1)S(1)} %collective-permute-done.5.refs_6_), channel_id=1, source_target_pairs={{0,1},{1,0},{2,3},{3,2},{4,5},{5,4},{6,7},{7,6},{8,9},{9,8},{10,11... | collective-permute-start | bytes 786440 | tf_op jit(solution)/shard_map/ppermute | solution.py:171
  59.5 3.4 %collective-permute-start.4 = (bf16[32,2,16,128]{3,2,1,0:T(8,128)(2,1)S(1)}, bf16[32,2,16,128]{3,2,1,0:T(8,128)(2,1)S(1)}, u32[]{:S(2)}, u32[]{:S(2)}) collective-permute-start(bf16[32,2,16,128]{3,2,1,0:T(8,128)(2,1)S(1)} %collective-permute-done.3.refs_4_), channel_id=1, source_target_pairs={{0,1},{1,0},{2,3},{3,2},{4,5},{5,4},{6,7},{7,6},{8,9},{9,8},{10,11... | collective-permute-start | bytes 786440 | tf_op jit(solution)/shard_map/ppermute | solution.py:171
  61.7 1.7 %collective-permute-start.2 = (bf16[32,2,16,128]{3,2,1,0:T(8,128)(2,1)S(1)}, bf16[32,2,16,128]{3,2,1,0:T(8,128)(2,1)S(1)}, u32[]{:S(2)}, u32[]{:S(2)}) collective-permute-start(bf16[32,2,16,128]{3,2,1,0:T(8,128)(2,1)S(1)} %collective-permute-done.1.refs_2_), channel_id=1, source_target_pairs={{0,1},{1,0},{2,3},{3,2},{4,5},{5,4},{6,7},{7,6},{8,9},{9,8},{10,11... | collective-permute-start | bytes 786440 | tf_op jit(solution)/shard_map/ppermute | solution.py:171

commit v2 on v1

--- a/solution.py
+++ b/solution.py
@@ -1,3 +1,4 @@
+import functools
 import math
 
 import jax
@@ -17,13 +18,14 @@
 TAPS = 16
 INPUTS_HERE = 8
 LANES = 128
-CHUNK = 128
+CHUNKS = (32, 96)
 PEERS = 32
 OWN = CHANNELS // PEERS
 ROWS = 2 * INPUTS_HERE
 STRIP_ROWS = PEERS * ROWS
 STRIPS = 8
-VMEM_LIMIT = 48 * 2**20
+VMEM_LIMIT = 60 * 2**20
+CORRELATE_LIMIT = 16 * 2**20
 
 
 def slab_table():
@@ -40,11 +42,11 @@
 def channelize_kernel(
     volt_hbm, taps_hbm, table_hbm, out_ref, volt, taps, table, filtered, product, turned, sems
 ):
-    parts = FRAMES // CHUNK
+    parts = len(CHUNKS)
     lands = []
     low = 0
     for part in range(parts):
-        high = (part + 1) * CHUNK + TAPS - 1
+        high = sum(CHUNKS[: part + 1]) + TAPS - 1
         span = pl.ds(low * FRAME_LEN, (high - low) * FRAME_LEN)
         lands.append(
             pltpu.make_async_copy(volt_hbm.at[:, span], volt.at[:, span], sems.at[part])
@@ -58,7 +60,7 @@
     table_copy.start()
     taps_copy.wait()
     for part in range(parts):
-        first = part * CHUNK
+        first, size = sum(CHUNKS[:part]), CHUNKS[part]
         lands[part].wait()
 
         def column(tile, carry):
@@ -69,12 +71,12 @@
             ]
             sums = {}
             before = None
-            for g in range(CHUNK + TAPS - 1):
+            for g in range(size + TAPS - 1):
                 start = pl.multiple_of((first + g) * FRAME_LEN + lane, LANES)
                 sample = volt[:, pl.ds(start, LANES)].astype(jnp.float32)
                 for t in range(TAPS):
                     f = g - t
-                    if 0 <= f < CHUNK:
+                    if 0 <= f < size:
                         term = weights[t] * sample
                         sums[f] = sums[f] + term if f in sums else term
                 f = g - (TAPS - 1)
@@ -102,7 +104,7 @@
 
 
 def channelize(volt, taps, table):
-    parts = FRAMES // CHUNK
+    parts = len(CHUNKS)
     return pl.pallas_call(
         channelize_kernel,
         out_shape=jax.ShapeDtypeStruct((CHANNELS, ROWS, FRAMES), jnp.bfloat16),
@@ -121,50 +123,53 @@
     )(volt, taps, table)
 
 
-def correlate_kernel(*refs):
-    blocks, out_hbm, stage, sems = refs[:STRIPS], refs[STRIPS], refs[STRIPS + 1], refs[STRIPS + 2]
+def correlate_kernel(places, held, *refs):
+    count = len(places)
+    left_ref, blocks = refs[0], refs[1 : count + 1]
+    out_hbm, stage, sems = refs[count + 1 + held :]
     z_hi = lax.axis_index("z_hi")
     core = lax.axis_index("core")
-    writes = [None, None]
-    step = 0
-    for ch in range(OWN):
-        left = blocks[0][:, ch].reshape(STRIP_ROWS, FRAMES)
-        for b in range(STRIPS):
-            slot = step % 2
-            strip = lax.rem(z_hi + STRIPS // 2 - b // 2, STRIPS // 2) * 2 + lax.rem(core + b % 2, 2)
-            right = blocks[b][:, ch].reshape(STRIP_ROWS, FRAMES)
+    writes = []
+    for (by, other), block in zip(places, blocks, strict=True):
+        strip = lax.rem(z_hi + 4 + by * (2 * core - 1), 4) * 2 + lax.rem(core + other, 2)
+        span = pl.ds(pl.multiple_of(strip * STRIP_ROWS, STRIP_ROWS), STRIP_ROWS)
+        for ch in range(OWN):
+            left = left_ref[:, ch].reshape(STRIP_ROWS, FRAMES)
+            right = block[:, ch].reshape(STRIP_ROWS, FRAMES)
             got = lax.dot_general(
                 left, right, (((1,), (1,)), ((), ())), preferred_element_type=jnp.float32
             )
-            if writes[slot] is not None:
-                writes[slot].wait()
+            slot = len(writes)
             stage[slot] = (got * (1.0 / FRAMES)).astype(jnp.bfloat16)
-            span = pl.ds(pl.multiple_of(strip * STRIP_ROWS, STRIP_ROWS), STRIP_ROWS)
-            writes[slot] = pltpu.make_async_copy(
-                stage.at[slot], out_hbm.at[ch, :, span], sems.at[slot]
-            )
-            writes[slot].start()
-            step += 1
+            write = pltpu.make_async_copy(stage.at[slot], out_hbm.at[ch, :, span], sems.at[slot])
+            write.start()
+            writes.append(write)
     for write in writes:
         write.wait()
 
 
-def correlate(blocks):
+def correlate(left, blocks, places, held=None):
+    count = len(blocks)
+    operands = [left, *blocks] + ([] if held is None else [held])
+    spaces = [pltpu.VMEM] * (count + 1) + ([] if held is None else [pl.ANY])
     return pl.pallas_call(
-        correlate_kernel,
+        functools.partial(correlate_kernel, places, 0 if held is None else 1),
         out_shape=jax.ShapeDtypeStruct((OWN, STRIP_ROWS, STRIPS * STRIP_ROWS), jnp.bfloat16),
-        in_specs=[pl.BlockSpec(memory_space=pltpu.VMEM)] * STRIPS,
+        in_specs=[pl.BlockSpec(memory_space=space) for space in spaces],
         out_specs=pl.BlockSpec(memory_space=pl.ANY),
         scratch_shapes=[
-            pltpu.VMEM((2, STRIP_ROWS, STRIP_ROWS), jnp.bfloat16),
-            pltpu.SemaphoreType.DMA((2,)),
+            pltpu.VMEM((OWN * count, STRIP_ROWS, STRIP_ROWS), jnp.bfloat16),
+            pltpu.SemaphoreType.DMA((OWN * count,)),
         ],
-        compiler_params=pltpu.CompilerParams(vmem_limit_bytes=VMEM_LIMIT),
-    )(*blocks)
-
-
-def shift(block, by):
-    return lax.ppermute(block, "z_hi", [(i, (i + by) % 4) for i in range(4)])
+        input_output_aliases={} if held is None else {count + 1: 0},
+        cost_estimate=pl.CostEstimate(flops=1, bytes_accessed=1, transcendentals=0),
+        compiler_params=pltpu.CompilerParams(vmem_limit_bytes=CORRELATE_LIMIT),
+    )(*operands)
+
+
+def onward(block):
+    way = [(2 * z + core, (z + (1, 3)[core]) % 4 * 2 + core) for z in range(4) for core in range(2)]
+    return lax.ppermute(block, ("z_hi", "core"), way)
 
 
 def swap(block):
@@ -175,11 +180,26 @@
     spectra = channelize(volt, taps, jnp.asarray(slab_table()))
     own = lax.all_to_all(spectra, ("z_lo", "x", "y"), split_axis=0, concat_axis=0, tiled=True)
     own = own.reshape(PEERS, OWN, ROWS, FRAMES)
-    blocks = []
-    for by in range(4):
-        block = shift(own, by) if by else own
-        blocks += [block, swap(block)]
-    return correlate(blocks)
+    sibling = swap(own)
+    first = onward(own)
+    out = correlate(own, [own, sibling], ((0, 0), (0, 1)))
+    sibling, out = lax.optimization_barrier((sibling, out))
+    second = onward(sibling)
+    third = onward(first)
+    first_other, second_other = swap(first), swap(second)
+    out = correlate(own, [first], ((1, 0),), out)
+    third, first_other, second, second_other, out = lax.optimization_barrier(
+        (third, first_other, second, second_other, out)
+    )
+    third_other = swap(third)
+    out = correlate(
+        own,
+        [first_other, second, second_other, third],
+        ((-1, 1), (1, 1), (-1, 0), (2, 0)),
+        out,
+    )
+    third_other, out = lax.optimization_barrier((third_other, out))
+    return correlate(own, [third_other], ((2, 1),), out)
 
 
 def solution(mesh):

time: 72.6 us -> 59.2 us (0.82)
  starting transfers between devices: 26.4 us -> 15.1 us
  local copies, waits for them, and re-layouts: 4.27 us -> 0 us
  waiting for transfers between devices: 5.76 us -> 8.18 us
  Pallas kernels: 20.7 us -> 19.9 us
    ppermute x4, starting transfers between devices: 18 us -> 2.21 us  [swap(): return lax.ppermute(block, 'core', [(0, 1), (1, 0)])]
    ppermute x3, starting transfers between devices: 8.38 us -> 12.8 us  [onward(): return lax.ppermute(block, ('z_hi', 'core'), way)]
    unnamed x6 -> x0, local copies, waits for them, and re-layouts: 4.27 us -> none
    ppermute x3, waiting for transfers between devices: 4.6 us -> 8.17 us  [onward(): return lax.ppermute(block, ('z_hi', 'core'), way)]
    pallas_call x1 -> x4, Pallas kernels: 9.01 us -> 6.58 us  [correlate(): pl.pallas_call(functools.partial(correlate_kernel, places, 0 if held is N...]
    pallas_call x1, Pallas kernels: 11.7 us -> 13.3 us  [channelize(): pl.pallas_call(channelize_kernel, out_shape=jax.ShapeDtypeStruct((CHANNEL...]
    ppermute x4, waiting for transfers between devices: 1.16 us -> 0.01 us  [swap(): return lax.ppermute(block, 'core', [(0, 1), (1, 0)])]
  transfers between devices with their start and end apart: 7 -> 7, of which waited for: 4 -> 3; matrix products, arithmetic and copies ran while one was open for 0% -> 0% of each run, Pallas kernels for 0% -> 9%
where the time goes in v2:
time: 59.2 us; the launch traced here: 58.7 us
  Pallas kernels  19.9 us (34%)
  blocking collectives  15.5 us (26%)
  starting transfers between devices  15.1 us (26%)
  waiting for transfers between devices  8.18 us (14%)
    all_to_all x1, blocking collectives, shards(): lax.all_to_all(spectra, ('z_lo', 'x', 'y'), split_axis=0, concat_axis=0,...  15.5 us
    pallas_call x1, Pallas kernels, channelize(): pl.pallas_call(channelize_kernel, out_shape=jax.ShapeDtypeStruct((CHANNEL...  13.3 us
    ppermute x3, starting transfers between devices, onward(): return lax.ppermute(block, ('z_hi', 'core'), way)  12.8 us
    ppermute x3, waiting for transfers between devices, onward(): return lax.ppermute(block, ('z_hi', 'core'), way)  8.17 us
    pallas_call x4, Pallas kernels, correlate(): pl.pallas_call(functools.partial(correlate_kernel, places, 0 if held is N...  6.58 us
    ppermute x4, starting transfers between devices, swap(): return lax.ppermute(block, 'core', [(0, 1), (1, 0)])  2.21 us
  transfers between devices with their start and end apart: 7, of which 3 were waited for; matrix products, arithmetic and copies ran while one was open for 0% of the time, Pallas kernels for 9%

profile of v2, /device:TPU:33, one launch (start us, length us, event | category | flops | bytes accessed | tf_op | source)
XLA Modules:
  0.0 58.7 jit_solution(9265508291283521990)
XLA Ops:
  0.0 13.3 %shard_map.37 = bf16[64,16,128]{2,1,0:T(8,128)(2,1)} custom-call(bf16[8,292864]{1,0:T(8,128)(2,1)} %volt_hbm.1, f32[16,2048]{1,0:T(8,128)} %taps_hbm.1, bf16[2048,128]{1,0:T(8,128)(2,1)} %constant.2.clone.table_hbm), custom_call_target="tpu_custom_call" | custom-call | tf_op jit(solution)/shard_map/pallas_call | solution.py:108
  13.4 15.5 %all_to_all.5 = bf16[64,16,128]{2,1,0:T(8,128)(2,1)S(1)} all-to-all(bf16[64,16,128]{2,1,0:T(8,128)(2,1)} %shard_map.37), channel_id=1, replica_groups=mesh['z_lo'=2,'x'=4,'y'=4,'z_hi'=4,'core'=2] {'z_lo','x','y'}, dimensions={0} | all-to-all | bytes 524288 | tf_op jit(solution)/shard_map/all_to_all | solution.py:181
  28.9 1.8 %collective-permute-start.3 = (bf16[32,2,16,128]{3,2,1,0:T(8,128)(2,1)S(1)}, bf16[32,2,16,128]{3,2,1,0:T(8,128)(2,1)S(1)}, u32[]{:S(2)}, u32[]{:S(2)}) collective-permute-start(bf16[32,2,16,128]{3,2,1,0:T(8,128)(2,1)S(1)} %bitcast.1), channel_id=1, source_target_pairs={{0,1},{1,0},{2,3},{3,2},{4,5},{5,4},{6,7},{7,6},{8,9},{9,8},{10,11... | collective-permute-start | bytes 786440 | tf_op jit(solution)/shard_map/ppermute | solution.py:176
  30.7 5.1 %collective-permute-start = (bf16[32,2,16,128]{3,2,1,0:T(8,128)(2,1)S(1)}, bf16[32,2,16,128]{3,2,1,0:T(8,128)(2,1)S(1)}, u32[]{:S(2)}, u32[]{:S(2)}) collective-permute-start(bf16[32,2,16,128]{3,2,1,0:T(8,128)(2,1)S(1)} %bitcast.2), channel_id=1, source_target_pairs={{0,2},{1,7},{2,4},{3,1},{4,6},{5,3},{6,0},{7,5},{8,10},{9,15},{10,... | collective-permute-start | bytes 786440 | tf_op jit(solution)/shard_map/ppermute | solution.py:172
  35.8 0.0 collective-permute-done.3.refs_2_
  35.8 1.6 %shard_map.38.refs_2_ = bf16[2,512,4096]{2,1,0:T(8,128)(2,1)} custom-call(bf16[32,2,16,128]{3,2,1,0:T(8,128)(2,1)S(1)} %bitcast.3, bf16[32,2,16,128]{3,2,1,0:T(8,128)(2,1)S(1)} %bitcast.4, bf16[32,2,16,128]{3,2,1,0:T(8,128)(2,1)S(1)} %collective-permute-done.3.refs_2_), custom_call_target="tpu_custom_call" | custom-call | flops 1 | bytes 1 | tf_op jit(solution)/shard_map/pallas_call | solution.py:155
  37.5 1.2 %collective-permute-start.4 = (bf16[32,2,16,128]{3,2,1,0:T(8,128)(2,1)S(1)}, bf16[32,2,16,128]{3,2,1,0:T(8,128)(2,1)S(1)}, u32[]{:S(2)}, u32[]{:S(2)}) collective-permute-start(bf16[32,2,16,128]{3,2,1,0:T(8,128)(2,1)S(1)} %collective-permute-done.3.refs_2_), channel_id=1, source_target_pairs={{0,2},{1,7},{2,4},{3,1},{4,6},{5,3},{6,0},{7,5},{8,10},{9,15},{10,... | collective-permute-start | bytes 786440 | tf_op jit(solution)/shard_map/ppermute | solution.py:172
  38.7 3.4 %collective-permute-done.refs_1_ = bf16[32,2,16,128]{3,2,1,0:T(8,128)(2,1)S(1)} collective-permute-done((bf16[32,2,16,128]{3,2,1,0:T(8,128)(2,1)S(1)}, bf16[32,2,16,128]{3,2,1,0:T(8,128)(2,1)S(1)}, u32[]{:S(2)}, u32[]{:S(2)}) %collective-permute-start) | collective-permute-done | bytes 262176 | tf_op jit(solution)/shard_map/ppermute | solution.py:172
  42.1 6.5 %collective-permute-start.1 = (bf16[32,2,16,128]{3,2,1,0:T(8,128)(2,1)S(1)}, bf16[32,2,16,128]{3,2,1,0:T(8,128)(2,1)S(1)}, u32[]{:S(2)}, u32[]{:S(2)}) collective-permute-start(bf16[32,2,16,128]{3,2,1,0:T(8,128)(2,1)S(1)} %collective-permute-done.refs_1_), channel_id=1, source_target_pairs={{0,2},{1,7},{2,4},{3,1},{4,6},{5,3},{6,0},{7,5},{8,10},{9,15},{10,... | collective-permute-start | bytes 786440 | tf_op jit(solution)/shard_map/ppermute | solution.py:172
  48.6 0.0 collective-permute-start.2
  48.6 1.5 %collective-permute-done.4.refs_2_ = bf16[32,2,16,128]{3,2,1,0:T(8,128)(2,1)S(1)} collective-permute-done((bf16[32,2,16,128]{3,2,1,0:T(8,128)(2,1)S(1)}, bf16[32,2,16,128]{3,2,1,0:T(8,128)(2,1)S(1)}, u32[]{:S(2)}, u32[]{:S(2)}) %collective-permute-start.4) | collective-permute-done | bytes 262176 | tf_op jit(solution)/shard_map/ppermute | solution.py:172
  50.1 0.0 collective-permute-start.5
  50.1 1.3 %shard_map.39.refs_5_ = bf16[2,512,4096]{2,1,0:T(8,128)(2,1)} custom-call(bf16[32,2,16,128]{3,2,1,0:T(8,128)(2,1)S(1)} %bitcast.5, bf16[32,2,16,128]{3,2,1,0:T(8,128)(2,1)S(1)} %collective-permute-done.refs_1_, bf16[2,512,4096]{2,1,0:T(8,128)(2,1)} %shard_map.38.refs_2_), custom_call_target="tpu_custom_call", output_to_operand_aliasing={{}: (2, {})} | custom-call | flops 1 | bytes 1 | tf_op jit(solution)/shard_map/pallas_call | solution.py:155
  51.4 3.3 %collective-permute-done.1.refs_4_ = bf16[32,2,16,128]{3,2,1,0:T(8,128)(2,1)S(1)} collective-permute-done((bf16[32,2,16,128]{3,2,1,0:T(8,128)(2,1)S(1)}, bf16[32,2,16,128]{3,2,1,0:T(8,128)(2,1)S(1)}, u32[]{:S(2)}, u32[]{:S(2)}) %collective-permute-start.1) | collective-permute-done | bytes 262176 | tf_op jit(solution)/shard_map/ppermute | solution.py:172
  54.6 0.0 collective-permute-done.2.refs_1_
  54.6 0.0 collective-permute-done.5.refs_3_
  54.7 0.4 collective-permute-start.6
  55.1 2.4 %shard_map.40.refs_2_ = bf16[2,512,4096]{2,1,0:T(8,128)(2,1)} custom-call(bf16[32,2,16,128]{3,2,1,0:T(8,128)(2,1)S(1)} %bitcast.6, bf16[32,2,16,128]{3,2,1,0:T(8,128)(2,1)S(1)} %collective-permute-done.2.refs_1_, bf16[32,2,16,128]{3,2,1,0:T(8,128)(2,1)S(1)} %collective-permute-done.4.refs_2_, ...), custom_call_target="tpu_custom_call", output_to_operand_aliasing={{}: (5, {})} | custom-call | flops 1 | bytes 1 | tf_op jit(solution)/shard_map/pallas_call | solution.py:155
  57.4 0.0 collective-permute-done.6.refs_1_
  57.4 1.3 %shard_map.41 = bf16[2,512,4096]{2,1,0:T(8,128)(2,1)} custom-call(bf16[32,2,16,128]{3,2,1,0:T(8,128)(2,1)S(1)} %bitcast.7, bf16[32,2,16,128]{3,2,1,0:T(8,128)(2,1)S(1)} %collective-permute-done.6.refs_1_, bf16[2,512,4096]{2,1,0:T(8,128)(2,1)} %shard_map.40.refs_2_), custom_call_target="tpu_custom_call", output_to_operand_aliasing={{}: (2, {})} | custom-call | flops 1 | bytes 1 | tf_op jit(solution)/shard_map/pallas_call | solution.py:155
Async XLA Ops:
  28.9 6.9 %collective-permute-start.3 = (bf16[32,2,16,128]{3,2,1,0:T(8,128)(2,1)S(1)}, bf16[32,2,16,128]{3,2,1,0:T(8,128)(2,1)S(1)}, u32[]{:S(2)}, u32[]{:S(2)}) collective-permute-start(bf16[32,2,16,128]{3,2,1,0:T(8,128)(2,1)S(1)} %bitcast.1), channel_id=1, source_target_pairs={{0,1},{1,0},{2,3},{3,2},{4,5},{5,4},{6,7},{7,6},{8,9},{9,8},{10,11... | collective-permute-start | bytes 786440 | tf_op jit(solution)/shard_map/ppermute | solution.py:176
  30.7 11.4 %collective-permute-start = (bf16[32,2,16,128]{3,2,1,0:T(8,128)(2,1)S(1)}, bf16[32,2,16,128]{3,2,1,0:T(8,128)(2,1)S(1)}, u32[]{:S(2)}, u32[]{:S(2)}) collective-permute-start(bf16[32,2,16,128]{3,2,1,0:T(8,128)(2,1)S(1)} %bitcast.2), channel_id=1, source_target_pairs={{0,2},{1,7},{2,4},{3,1},{4,6},{5,3},{6,0},{7,5},{8,10},{9,15},{10,... | collective-permute-start | bytes 786440 | tf_op jit(solution)/shard_map/ppermute | solution.py:172
  37.5 12.6 %collective-permute-start.4 = (bf16[32,2,16,128]{3,2,1,0:T(8,128)(2,1)S(1)}, bf16[32,2,16,128]{3,2,1,0:T(8,128)(2,1)S(1)}, u32[]{:S(2)}, u32[]{:S(2)}) collective-permute-start(bf16[32,2,16,128]{3,2,1,0:T(8,128)(2,1)S(1)} %collective-permute-done.3.refs_2_), channel_id=1, source_target_pairs={{0,2},{1,7},{2,4},{3,1},{4,6},{5,3},{6,0},{7,5},{8,10},{9,15},{10,... | collective-permute-start | bytes 786440 | tf_op jit(solution)/shard_map/ppermute | solution.py:172
  42.1 12.6 %collective-permute-start.1 = (bf16[32,2,16,128]{3,2,1,0:T(8,128)(2,1)S(1)}, bf16[32,2,16,128]{3,2,1,0:T(8,128)(2,1)S(1)}, u32[]{:S(2)}, u32[]{:S(2)}) collective-permute-start(bf16[32,2,16,128]{3,2,1,0:T(8,128)(2,1)S(1)} %collective-permute-done.refs_1_), channel_id=1, source_target_pairs={{0,2},{1,7},{2,4},{3,1},{4,6},{5,3},{6,0},{7,5},{8,10},{9,15},{10,... | collective-permute-start | bytes 786440 | tf_op jit(solution)/shard_map/ppermute | solution.py:172
  48.6 6.1 %collective-permute-start.2 = (bf16[32,2,16,128]{3,2,1,0:T(8,128)(2,1)S(1)}, bf16[32,2,16,128]{3,2,1,0:T(8,128)(2,1)S(1)}, u32[]{:S(2)}, u32[]{:S(2)}) collective-permute-start(bf16[32,2,16,128]{3,2,1,0:T(8,128)(2,1)S(1)} %collective-permute-done.refs_1_), channel_id=1, source_target_pairs={{0,1},{1,0},{2,3},{3,2},{4,5},{5,4},{6,7},{7,6},{8,9},{9,8},{10,11... | collective-permute-start | bytes 786440 | tf_op jit(solution)/shard_map/ppermute | solution.py:176
  50.1 4.6 %collective-permute-start.5 = (bf16[32,2,16,128]{3,2,1,0:T(8,128)(2,1)S(1)}, bf16[32,2,16,128]{3,2,1,0:T(8,128)(2,1)S(1)}, u32[]{:S(2)}, u32[]{:S(2)}) collective-permute-start(bf16[32,2,16,128]{3,2,1,0:T(8,128)(2,1)S(1)} %collective-permute-done.4.refs_2_), channel_id=1, source_target_pairs={{0,1},{1,0},{2,3},{3,2},{4,5},{5,4},{6,7},{7,6},{8,9},{9,8},{10,11... | collective-permute-start | bytes 786440 | tf_op jit(solution)/shard_map/ppermute | solution.py:176
  54.7 2.8 %collective-permute-start.6 = (bf16[32,2,16,128]{3,2,1,0:T(8,128)(2,1)S(1)}, bf16[32,2,16,128]{3,2,1,0:T(8,128)(2,1)S(1)}, u32[]{:S(2)}, u32[]{:S(2)}) collective-permute-start(bf16[32,2,16,128]{3,2,1,0:T(8,128)(2,1)S(1)} %collective-permute-done.1.refs_4_), channel_id=1, source_target_pairs={{0,1},{1,0},{2,3},{3,2},{4,5},{5,4},{6,7},{7,6},{8,9},{9,8},{10,11... | collective-permute-start | bytes 786440 | tf_op jit(solution)/shard_map/ppermute | solution.py:176

commit v3 on v2

--- a/solution.py
+++ b/solution.py
@@ -18,7 +18,7 @@
 TAPS = 16
 INPUTS_HERE = 8
 LANES = 128
-CHUNKS = (32, 96)
+LEAST = 4
 PEERS = 32
 OWN = CHANNELS // PEERS
 ROWS = 2 * INPUTS_HERE
@@ -39,56 +39,97 @@
     ).astype(ml_dtypes.bfloat16)
 
 
+def filter_of(taps, sample, least):
+    known = {}
+    if len(taps) <= least:
+
+        def plain(n):
+            if n not in known:
+                total = None
+                for s, tap in enumerate(taps):
+                    value = sample(n - s)
+                    if value is not None:
+                        term = tap * value
+                        total = term if total is None else total + term
+                known[n] = total
+            return known[n]
+
+        return plain
+
+    both = {}
+
+    def even(m):
+        return sample(2 * m)
+
+    def odd(m):
+        return sample(2 * m + 1)
+
+    def joined(m):
+        if m not in both:
+            left, right = even(m), odd(m)
+            both[m] = right if left is None else left + right
+        return both[m]
+
+    even_taps, odd_taps = taps[0::2], taps[1::2]
+    joined_taps = [left + right for left, right in zip(even_taps, odd_taps, strict=True)]
+    of_even = filter_of(even_taps, even, least)
+    of_odd = filter_of(odd_taps, odd, least)
+    of_joined = filter_of(joined_taps, joined, least)
+
+    def split(n):
+        if n not in known:
+            m = n // 2
+            if n % 2 == 0:
+                known[n] = of_even(m) + of_odd(m - 1)
+            else:
+                known[n] = (of_joined(m) - of_even(m)) - of_odd(m)
+        return known[n]
+
+    return split
+
+
 def channelize_kernel(
     volt_hbm, taps_hbm, table_hbm, out_ref, volt, taps, table, filtered, product, turned, sems
 ):
-    parts = len(CHUNKS)
-    lands = []
-    low = 0
-    for part in range(parts):
-        high = sum(CHUNKS[: part + 1]) + TAPS - 1
-        span = pl.ds(low * FRAME_LEN, (high - low) * FRAME_LEN)
-        lands.append(
-            pltpu.make_async_copy(volt_hbm.at[:, span], volt.at[:, span], sems.at[part])
+    tiles = FRAME_LEN // LANES
+
+    def landing(tile):
+        span = pl.ds(pl.multiple_of(tile * LANES, LANES), LANES)
+        return pltpu.make_async_copy(
+            volt_hbm.at[:, :, span], volt.at[:, :, span], sems.at[tile]
         )
-        low = high
-    taps_copy = pltpu.make_async_copy(taps_hbm, taps, sems.at[parts])
-    table_copy = pltpu.make_async_copy(table_hbm, table, sems.at[parts + 1])
+
+    taps_copy = pltpu.make_async_copy(taps_hbm, taps, sems.at[tiles])
+    table_copy = pltpu.make_async_copy(table_hbm, table, sems.at[tiles + 1])
     taps_copy.start()
-    for land in lands:
-        land.start()
+    for tile in range(tiles):
+        landing(tile).start()
     table_copy.start()
     taps_copy.wait()
-    for part in range(parts):
-        first, size = sum(CHUNKS[:part]), CHUNKS[part]
-        lands[part].wait()
-
-        def column(tile, carry):
-            lane = pl.multiple_of(tile * LANES, LANES)
-            weights = [
-                jnp.broadcast_to(taps[pl.ds(t, 1), pl.ds(lane, LANES)], (INPUTS_HERE, LANES))
-                for t in range(TAPS)
-            ]
-            sums = {}
-            before = None
-            for g in range(size + TAPS - 1):
-                start = pl.multiple_of((first + g) * FRAME_LEN + lane, LANES)
-                sample = volt[:, pl.ds(start, LANES)].astype(jnp.float32)
-                for t in range(TAPS):
-                    f = g - t
-                    if 0 <= f < size:
-                        term = weights[t] * sample
-                        sums[f] = sums[f] + term if f in sums else term
-                f = g - (TAPS - 1)
-                if f >= 0 and f % 2 == 0:
-                    before = sums.pop(f)
-                elif f >= 0:
-                    pair = jnp.concatenate([before, sums.pop(f)], axis=0)
-                    rows = pl.ds((first + f - 1) * INPUTS_HERE, 2 * INPUTS_HERE)
-                    filtered[rows, pl.ds(lane, LANES)] = pair.astype(jnp.bfloat16)
-            return carry
-
-        lax.fori_loop(0, FRAME_LEN // LANES, column, 0)
+
+    def column(tile, carry):
+        landing(tile).wait()
+        lane = pl.ds(pl.multiple_of(tile * LANES, LANES), LANES)
+        weights = [
+            jnp.broadcast_to(taps[pl.ds(TAPS - 1 - j, 1), lane], (INPUTS_HERE, LANES))
+            for j in range(TAPS)
+        ]
+        loaded = {}
+
+        def sample(n):
+            if n < 1:
+                return None
+            if n not in loaded:
+                loaded[n] = volt[n - 1, :, lane].astype(jnp.float32)
+            return loaded[n]
+
+        output = filter_of(weights, sample, LEAST)
+        for f in range(0, FRAMES, 2):
+            pair = jnp.concatenate([output(f + TAPS), output(f + TAPS + 1)], axis=0)
+            filtered[f * INPUTS_HERE : (f + 2) * INPUTS_HERE, lane] = pair.astype(jnp.bfloat16)
+        return carry
+
+    lax.fori_loop(0, tiles, column, 0)
     table_copy.wait()
     product[...] = jnp.dot(filtered[...], table[...], preferred_element_type=jnp.float32)
     for i in range(INPUTS_HERE):
@@ -104,23 +145,23 @@
 
 
 def channelize(volt, taps, table):
-    parts = len(CHUNKS)
+    framed = jnp.transpose(volt.reshape(INPUTS_HERE, -1, FRAME_LEN), (1, 0, 2))
     return pl.pallas_call(
         channelize_kernel,
         out_shape=jax.ShapeDtypeStruct((CHANNELS, ROWS, FRAMES), jnp.bfloat16),
         in_specs=[pl.BlockSpec(memory_space=pl.ANY)] * 3,
         out_specs=pl.BlockSpec(memory_space=pltpu.VMEM),
         scratch_shapes=[
-            pltpu.VMEM(volt.shape, jnp.bfloat16),
+            pltpu.VMEM(framed.shape, jnp.bfloat16),
             pltpu.VMEM((TAPS, FRAME_LEN), jnp.float32),
             pltpu.VMEM((FRAME_LEN, 2 * CHANNELS), jnp.bfloat16),
             pltpu.VMEM((FRAMES * INPUTS_HERE, FRAME_LEN), jnp.bfloat16),
             pltpu.VMEM((FRAMES * INPUTS_HERE, 2 * CHANNELS), jnp.float32),
             pltpu.VMEM((FRAMES * INPUTS_HERE, FRAMES), jnp.float32),
-            pltpu.SemaphoreType.DMA((parts + 2,)),
+            pltpu.SemaphoreType.DMA((FRAME_LEN // LANES + 2,)),
         ],
         compiler_params=pltpu.CompilerParams(vmem_limit_bytes=VMEM_LIMIT),
-    )(volt, taps, table)
+    )(framed, taps, table)
 
 
 def correlate_kernel(places, held, *refs):

time: 59.2 us -> 56.3 us (0.951)
  Pallas kernels: 19.9 us -> 17 us
    pallas_call x1, Pallas kernels: 13.3 us -> 10.4 us  [channelize(): pl.pallas_call(channelize_kernel, out_shape=jax.ShapeDtypeStruct((CHANNEL...]
where the time goes in v3:
time: 56.3 us; the launch traced here: 55.8 us
  Pallas kernels  17 us (30%)
  blocking collectives  15.5 us (28%)
  starting transfers between devices  15.1 us (27%)
  waiting for transfers between devices  8.19 us (15%)
    all_to_all x1, blocking collectives, shards(): lax.all_to_all(spectra, ('z_lo', 'x', 'y'), split_axis=0, concat_axis=0,...  15.5 us
    ppermute x3, starting transfers between devices, onward(): return lax.ppermute(block, ('z_hi', 'core'), way)  12.8 us
    pallas_call x1, Pallas kernels, channelize(): pl.pallas_call(channelize_kernel, out_shape=jax.ShapeDtypeStruct((CHANNEL...  10.4 us
    ppermute x3, waiting for transfers between devices, onward(): return lax.ppermute(block, ('z_hi', 'core'), way)  8.18 us
    pallas_call x4, Pallas kernels, correlate(): pl.pallas_call(functools.partial(correlate_kernel, places, 0 if held is N...  6.58 us
    ppermute x4, starting transfers between devices, swap(): return lax.ppermute(block, 'core', [(0, 1), (1, 0)])  2.21 us
  transfers between devices with their start and end apart: 7, of which 3 were waited for; matrix products, arithmetic and copies ran while one was open for 0% of the time, Pallas kernels for 9%

profile of v3, /device:TPU:33, one launch (start us, length us, event | category | flops | bytes accessed | tf_op | source)
XLA Modules:
  0.0 55.8 jit_solution(1042360193564247417)
XLA Ops:
  0.0 10.4 %shard_map.37 = bf16[64,16,128]{2,1,0:T(8,128)(2,1)} custom-call(bf16[143,8,2048]{2,1,0:T(8,128)(2,1)} %bitcast.11, f32[16,2048]{1,0:T(8,128)} %taps_hbm.1, bf16[2048,128]{1,0:T(8,128)(2,1)} %constant.2.clone.table_hbm), custom_call_target="tpu_custom_call" | custom-call | tf_op jit(solution)/shard_map/pallas_call | solution.py:149
  10.4 15.5 %all_to_all.5 = bf16[64,16,128]{2,1,0:T(8,128)(2,1)S(1)} all-to-all(bf16[64,16,128]{2,1,0:T(8,128)(2,1)} %shard_map.37), channel_id=1, replica_groups=mesh['z_lo'=2,'x'=4,'y'=4,'z_hi'=4,'core'=2] {'z_lo','x','y'}, dimensions={0} | all-to-all | bytes 524288 | tf_op jit(solution)/shard_map/all_to_all | solution.py:222
  25.9 1.8 %collective-permute-start.3 = (bf16[32,2,16,128]{3,2,1,0:T(8,128)(2,1)S(1)}, bf16[32,2,16,128]{3,2,1,0:T(8,128)(2,1)S(1)}, u32[]{:S(2)}, u32[]{:S(2)}) collective-permute-start(bf16[32,2,16,128]{3,2,1,0:T(8,128)(2,1)S(1)} %bitcast.4), channel_id=1, source_target_pairs={{0,1},{1,0},{2,3},{3,2},{4,5},{5,4},{6,7},{7,6},{8,9},{9,8},{10,11... | collective-permute-start | bytes 786440 | tf_op jit(solution)/shard_map/ppermute | solution.py:217
  27.7 5.1 %collective-permute-start = (bf16[32,2,16,128]{3,2,1,0:T(8,128)(2,1)S(1)}, bf16[32,2,16,128]{3,2,1,0:T(8,128)(2,1)S(1)}, u32[]{:S(2)}, u32[]{:S(2)}) collective-permute-start(bf16[32,2,16,128]{3,2,1,0:T(8,128)(2,1)S(1)} %bitcast.5), channel_id=1, source_target_pairs={{0,2},{1,7},{2,4},{3,1},{4,6},{5,3},{6,0},{7,5},{8,10},{9,15},{10,... | collective-permute-start | bytes 786440 | tf_op jit(solution)/shard_map/ppermute | solution.py:213
  32.9 0.0 collective-permute-done.3.refs_2_
  32.9 1.6 %shard_map.38.refs_2_ = bf16[2,512,4096]{2,1,0:T(8,128)(2,1)} custom-call(bf16[32,2,16,128]{3,2,1,0:T(8,128)(2,1)S(1)} %bitcast.6, bf16[32,2,16,128]{3,2,1,0:T(8,128)(2,1)S(1)} %bitcast.7, bf16[32,2,16,128]{3,2,1,0:T(8,128)(2,1)S(1)} %collective-permute-done.3.refs_2_), custom_call_target="tpu_custom_call" | custom-call | flops 1 | bytes 1 | tf_op jit(solution)/shard_map/pallas_call | solution.py:196
  34.5 1.2 %collective-permute-start.4 = (bf16[32,2,16,128]{3,2,1,0:T(8,128)(2,1)S(1)}, bf16[32,2,16,128]{3,2,1,0:T(8,128)(2,1)S(1)}, u32[]{:S(2)}, u32[]{:S(2)}) collective-permute-start(bf16[32,2,16,128]{3,2,1,0:T(8,128)(2,1)S(1)} %collective-permute-done.3.refs_2_), channel_id=1, source_target_pairs={{0,2},{1,7},{2,4},{3,1},{4,6},{5,3},{6,0},{7,5},{8,10},{9,15},{10,... | collective-permute-start | bytes 786440 | tf_op jit(solution)/shard_map/ppermute | solution.py:213
  35.8 3.4 %collective-permute-done.refs_1_ = bf16[32,2,16,128]{3,2,1,0:T(8,128)(2,1)S(1)} collective-permute-done((bf16[32,2,16,128]{3,2,1,0:T(8,128)(2,1)S(1)}, bf16[32,2,16,128]{3,2,1,0:T(8,128)(2,1)S(1)}, u32[]{:S(2)}, u32[]{:S(2)}) %collective-permute-start) | collective-permute-done | bytes 262176 | tf_op jit(solution)/shard_map/ppermute | solution.py:213
  39.2 6.5 %collective-permute-start.1 = (bf16[32,2,16,128]{3,2,1,0:T(8,128)(2,1)S(1)}, bf16[32,2,16,128]{3,2,1,0:T(8,128)(2,1)S(1)}, u32[]{:S(2)}, u32[]{:S(2)}) collective-permute-start(bf16[32,2,16,128]{3,2,1,0:T(8,128)(2,1)S(1)} %collective-permute-done.refs_1_), channel_id=1, source_target_pairs={{0,2},{1,7},{2,4},{3,1},{4,6},{5,3},{6,0},{7,5},{8,10},{9,15},{10,... | collective-permute-start | bytes 786440 | tf_op jit(solution)/shard_map/ppermute | solution.py:213
  45.6 0.0 collective-permute-start.2
  45.6 1.5 %collective-permute-done.4.refs_2_ = bf16[32,2,16,128]{3,2,1,0:T(8,128)(2,1)S(1)} collective-permute-done((bf16[32,2,16,128]{3,2,1,0:T(8,128)(2,1)S(1)}, bf16[32,2,16,128]{3,2,1,0:T(8,128)(2,1)S(1)}, u32[]{:S(2)}, u32[]{:S(2)}) %collective-permute-start.4) | collective-permute-done | bytes 262176 | tf_op jit(solution)/shard_map/ppermute | solution.py:213
  47.1 0.0 collective-permute-start.5
  47.1 1.3 %shard_map.39.refs_5_ = bf16[2,512,4096]{2,1,0:T(8,128)(2,1)} custom-call(bf16[32,2,16,128]{3,2,1,0:T(8,128)(2,1)S(1)} %bitcast.8, bf16[32,2,16,128]{3,2,1,0:T(8,128)(2,1)S(1)} %collective-permute-done.refs_1_, bf16[2,512,4096]{2,1,0:T(8,128)(2,1)} %shard_map.38.refs_2_), custom_call_target="tpu_custom_call", output_to_operand_aliasing={{}: (2, {})} | custom-call | flops 1 | bytes 1 | tf_op jit(solution)/shard_map/pallas_call | solution.py:196
  48.4 3.3 %collective-permute-done.1.refs_4_ = bf16[32,2,16,128]{3,2,1,0:T(8,128)(2,1)S(1)} collective-permute-done((bf16[32,2,16,128]{3,2,1,0:T(8,128)(2,1)S(1)}, bf16[32,2,16,128]{3,2,1,0:T(8,128)(2,1)S(1)}, u32[]{:S(2)}, u32[]{:S(2)}) %collective-permute-start.1) | collective-permute-done | bytes 262176 | tf_op jit(solution)/shard_map/ppermute | solution.py:213
  51.7 0.0 collective-permute-done.2.refs_1_
  51.7 0.0 collective-permute-done.5.refs_3_
  51.7 0.4 collective-permute-start.6
  52.1 2.4 %shard_map.40.refs_2_ = bf16[2,512,4096]{2,1,0:T(8,128)(2,1)} custom-call(bf16[32,2,16,128]{3,2,1,0:T(8,128)(2,1)S(1)} %bitcast.9, bf16[32,2,16,128]{3,2,1,0:T(8,128)(2,1)S(1)} %collective-permute-done.2.refs_1_, bf16[32,2,16,128]{3,2,1,0:T(8,128)(2,1)S(1)} %collective-permute-done.4.refs_2_, ...), custom_call_target="tpu_custom_call", output_to_operand_aliasing={{}: (5, {})} | custom-call | flops 1 | bytes 1 | tf_op jit(solution)/shard_map/pallas_call | solution.py:196
  54.5 0.0 collective-permute-done.6.refs_1_
  54.5 1.3 %shard_map.41 = bf16[2,512,4096]{2,1,0:T(8,128)(2,1)} custom-call(bf16[32,2,16,128]{3,2,1,0:T(8,128)(2,1)S(1)} %bitcast.10, bf16[32,2,16,128]{3,2,1,0:T(8,128)(2,1)S(1)} %collective-permute-done.6.refs_1_, bf16[2,512,4096]{2,1,0:T(8,128)(2,1)} %shard_map.40.refs_2_), custom_call_target="tpu_custom_call", output_to_operand_aliasing={{}: (2, {})} | custom-call | flops 1 | bytes 1 | tf_op jit(solution)/shard_map/pallas_call | solution.py:196
Async XLA Ops:
  25.9 6.9 %collective-permute-start.3 = (bf16[32,2,16,128]{3,2,1,0:T(8,128)(2,1)S(1)}, bf16[32,2,16,128]{3,2,1,0:T(8,128)(2,1)S(1)}, u32[]{:S(2)}, u32[]{:S(2)}) collective-permute-start(bf16[32,2,16,128]{3,2,1,0:T(8,128)(2,1)S(1)} %bitcast.4), channel_id=1, source_target_pairs={{0,1},{1,0},{2,3},{3,2},{4,5},{5,4},{6,7},{7,6},{8,9},{9,8},{10,11... | collective-permute-start | bytes 786440 | tf_op jit(solution)/shard_map/ppermute | solution.py:217
  27.7 11.4 %collective-permute-start = (bf16[32,2,16,128]{3,2,1,0:T(8,128)(2,1)S(1)}, bf16[32,2,16,128]{3,2,1,0:T(8,128)(2,1)S(1)}, u32[]{:S(2)}, u32[]{:S(2)}) collective-permute-start(bf16[32,2,16,128]{3,2,1,0:T(8,128)(2,1)S(1)} %bitcast.5), channel_id=1, source_target_pairs={{0,2},{1,7},{2,4},{3,1},{4,6},{5,3},{6,0},{7,5},{8,10},{9,15},{10,... | collective-permute-start | bytes 786440 | tf_op jit(solution)/shard_map/ppermute | solution.py:213
  34.5 12.6 %collective-permute-start.4 = (bf16[32,2,16,128]{3,2,1,0:T(8,128)(2,1)S(1)}, bf16[32,2,16,128]{3,2,1,0:T(8,128)(2,1)S(1)}, u32[]{:S(2)}, u32[]{:S(2)}) collective-permute-start(bf16[32,2,16,128]{3,2,1,0:T(8,128)(2,1)S(1)} %collective-permute-done.3.refs_2_), channel_id=1, source_target_pairs={{0,2},{1,7},{2,4},{3,1},{4,6},{5,3},{6,0},{7,5},{8,10},{9,15},{10,... | collective-permute-start | bytes 786440 | tf_op jit(solution)/shard_map/ppermute | solution.py:213
  39.2 12.6 %collective-permute-start.1 = (bf16[32,2,16,128]{3,2,1,0:T(8,128)(2,1)S(1)}, bf16[32,2,16,128]{3,2,1,0:T(8,128)(2,1)S(1)}, u32[]{:S(2)}, u32[]{:S(2)}) collective-permute-start(bf16[32,2,16,128]{3,2,1,0:T(8,128)(2,1)S(1)} %collective-permute-done.refs_1_), channel_id=1, source_target_pairs={{0,2},{1,7},{2,4},{3,1},{4,6},{5,3},{6,0},{7,5},{8,10},{9,15},{10,... | collective-permute-start | bytes 786440 | tf_op jit(solution)/shard_map/ppermute | solution.py:213
  45.6 6.1 %collective-permute-start.2 = (bf16[32,2,16,128]{3,2,1,0:T(8,128)(2,1)S(1)}, bf16[32,2,16,128]{3,2,1,0:T(8,128)(2,1)S(1)}, u32[]{:S(2)}, u32[]{:S(2)}) collective-permute-start(bf16[32,2,16,128]{3,2,1,0:T(8,128)(2,1)S(1)} %collective-permute-done.refs_1_), channel_id=1, source_target_pairs={{0,1},{1,0},{2,3},{3,2},{4,5},{5,4},{6,7},{7,6},{8,9},{9,8},{10,11... | collective-permute-start | bytes 786440 | tf_op jit(solution)/shard_map/ppermute | solution.py:217
  47.1 4.6 %collective-permute-start.5 = (bf16[32,2,16,128]{3,2,1,0:T(8,128)(2,1)S(1)}, bf16[32,2,16,128]{3,2,1,0:T(8,128)(2,1)S(1)}, u32[]{:S(2)}, u32[]{:S(2)}) collective-permute-start(bf16[32,2,16,128]{3,2,1,0:T(8,128)(2,1)S(1)} %collective-permute-done.4.refs_2_), channel_id=1, source_target_pairs={{0,1},{1,0},{2,3},{3,2},{4,5},{5,4},{6,7},{7,6},{8,9},{9,8},{10,11... | collective-permute-start | bytes 786440 | tf_op jit(solution)/shard_map/ppermute | solution.py:217
  51.7 2.8 %collective-permute-start.6 = (bf16[32,2,16,128]{3,2,1,0:T(8,128)(2,1)S(1)}, bf16[32,2,16,128]{3,2,1,0:T(8,128)(2,1)S(1)}, u32[]{:S(2)}, u32[]{:S(2)}) collective-permute-start(bf16[32,2,16,128]{3,2,1,0:T(8,128)(2,1)S(1)} %collective-permute-done.1.refs_4_), channel_id=1, source_target_pairs={{0,1},{1,0},{2,3},{3,2},{4,5},{5,4},{6,7},{7,6},{8,9},{9,8},{10,11... | collective-permute-start | bytes 786440 | tf_op jit(solution)/shard_map/ppermute | solution.py:217

commit v4 on v3

--- a/solution.py
+++ b/solution.py
@@ -228,17 +228,12 @@
     second = onward(sibling)
     third = onward(first)
     first_other, second_other = swap(first), swap(second)
-    out = correlate(own, [first], ((1, 0),), out)
-    third, first_other, second, second_other, out = lax.optimization_barrier(
-        (third, first_other, second, second_other, out)
+    out = correlate(
+        own, [first, first_other, second], ((1, 0), (-1, 1), (1, 1)), out
     )
+    third, second_other, out = lax.optimization_barrier((third, second_other, out))
     third_other = swap(third)
-    out = correlate(
-        own,
-        [first_other, second, second_other, third],
-        ((-1, 1), (1, 1), (-1, 0), (2, 0)),
-        out,
-    )
+    out = correlate(own, [second_other, third], ((-1, 0), (2, 0)), out)
     third_other, out = lax.optimization_barrier((third_other, out))
     return correlate(own, [third_other], ((2, 1),), out)
 

time: 56.3 us -> 55.5 us (0.986)
  waiting for transfers between devices: 8.19 us -> 5.69 us
  starting transfers between devices: 15.1 us -> 17.1 us
    ppermute x4, starting transfers between devices: 2.21 us -> 5.68 us  [swap(): return lax.ppermute(block, 'core', [(0, 1), (1, 0)])]
    ppermute x3, waiting for transfers between devices: 8.18 us -> 5.68 us  [onward(): return lax.ppermute(block, ('z_hi', 'core'), way)]
    ppermute x3, starting transfers between devices: 12.8 us -> 11.5 us  [onward(): return lax.ppermute(block, ('z_hi', 'core'), way)]
  transfers between devices with their start and end apart: 7 -> 7, of which waited for: 3 -> 3; matrix products, arithmetic and copies ran while one was open for 0% -> 0% of each run, Pallas kernels for 9% -> 10%
where the time goes in v4:
time: 55.5 us; the launch traced here: 55.4 us
  starting transfers between devices  17.1 us (31%)
  Pallas kernels  17 us (31%)
  blocking collectives  15.5 us (28%)
  waiting for transfers between devices  5.69 us (10%)
    all_to_all x1, blocking collectives, shards(): lax.all_to_all(spectra, ('z_lo', 'x', 'y'), split_axis=0, concat_axis=0,...  15.5 us
    ppermute x3, starting transfers between devices, onward(): return lax.ppermute(block, ('z_hi', 'core'), way)  11.5 us
    pallas_call x1, Pallas kernels, channelize(): pl.pallas_call(channelize_kernel, out_shape=jax.ShapeDtypeStruct((CHANNEL...  10.4 us
    pallas_call x4, Pallas kernels, correlate(): pl.pallas_call(functools.partial(correlate_kernel, places, 0 if held is N...  6.58 us
    ppermute x4, starting transfers between devices, swap(): return lax.ppermute(block, 'core', [(0, 1), (1, 0)])  5.68 us
    ppermute x3, waiting for transfers between devices, onward(): return lax.ppermute(block, ('z_hi', 'core'), way)  5.68 us
  transfers between devices with their start and end apart: 7, of which 3 were waited for; matrix products, arithmetic and copies ran while one was open for 0% of the time, Pallas kernels for 10%

profile of v4, /device:TPU:33, one launch (start us, length us, event | category | flops | bytes accessed | tf_op | source)
XLA Modules:
  0.0 55.4 jit_solution(2096991041763298329)
XLA Ops:
  0.0 10.4 %shard_map.37 = bf16[64,16,128]{2,1,0:T(8,128)(2,1)} custom-call(bf16[143,8,2048]{2,1,0:T(8,128)(2,1)} %bitcast.11, f32[16,2048]{1,0:T(8,128)} %taps_hbm.1, bf16[2048,128]{1,0:T(8,128)(2,1)} %constant.2.clone.table_hbm), custom_call_target="tpu_custom_call" | custom-call | tf_op jit(solution)/shard_map/pallas_call | solution.py:149
  10.4 15.5 %all_to_all.5 = bf16[64,16,128]{2,1,0:T(8,128)(2,1)S(1)} all-to-all(bf16[64,16,128]{2,1,0:T(8,128)(2,1)} %shard_map.37), channel_id=1, replica_groups=mesh['z_lo'=2,'x'=4,'y'=4,'z_hi'=4,'core'=2] {'z_lo','x','y'}, dimensions={0} | all-to-all | bytes 524288 | tf_op jit(solution)/shard_map/all_to_all | solution.py:222
  25.9 1.8 %collective-permute-start.2 = (bf16[32,2,16,128]{3,2,1,0:T(8,128)(2,1)S(1)}, bf16[32,2,16,128]{3,2,1,0:T(8,128)(2,1)S(1)}, u32[]{:S(2)}, u32[]{:S(2)}) collective-permute-start(bf16[32,2,16,128]{3,2,1,0:T(8,128)(2,1)S(1)} %bitcast.4), channel_id=1, source_target_pairs={{0,1},{1,0},{2,3},{3,2},{4,5},{5,4},{6,7},{7,6},{8,9},{9,8},{10,11... | collective-permute-start | bytes 786440 | tf_op jit(solution)/shard_map/ppermute | solution.py:217
  27.7 5.1 %collective-permute-start = (bf16[32,2,16,128]{3,2,1,0:T(8,128)(2,1)S(1)}, bf16[32,2,16,128]{3,2,1,0:T(8,128)(2,1)S(1)}, u32[]{:S(2)}, u32[]{:S(2)}) collective-permute-start(bf16[32,2,16,128]{3,2,1,0:T(8,128)(2,1)S(1)} %bitcast.5), channel_id=1, source_target_pairs={{0,2},{1,7},{2,4},{3,1},{4,6},{5,3},{6,0},{7,5},{8,10},{9,15},{10,... | collective-permute-start | bytes 786440 | tf_op jit(solution)/shard_map/ppermute | solution.py:213
  32.9 0.0 collective-permute-done.2.refs_2_
  32.9 1.6 %shard_map.38.refs_4_ = bf16[2,512,4096]{2,1,0:T(8,128)(2,1)} custom-call(bf16[32,2,16,128]{3,2,1,0:T(8,128)(2,1)S(1)} %bitcast.6, bf16[32,2,16,128]{3,2,1,0:T(8,128)(2,1)S(1)} %bitcast.7, bf16[32,2,16,128]{3,2,1,0:T(8,128)(2,1)S(1)} %collective-permute-done.2.refs_2_), custom_call_target="tpu_custom_call" | custom-call | flops 1 | bytes 1 | tf_op jit(solution)/shard_map/pallas_call | solution.py:196
  34.5 1.2 %collective-permute-start.3 = (bf16[32,2,16,128]{3,2,1,0:T(8,128)(2,1)S(1)}, bf16[32,2,16,128]{3,2,1,0:T(8,128)(2,1)S(1)}, u32[]{:S(2)}, u32[]{:S(2)}) collective-permute-start(bf16[32,2,16,128]{3,2,1,0:T(8,128)(2,1)S(1)} %collective-permute-done.2.refs_2_), channel_id=1, source_target_pairs={{0,2},{1,7},{2,4},{3,1},{4,6},{5,3},{6,0},{7,5},{8,10},{9,15},{10,... | collective-permute-start | bytes 786440 | tf_op jit(solution)/shard_map/ppermute | solution.py:213
  35.8 3.4 %collective-permute-done.refs_1_ = bf16[32,2,16,128]{3,2,1,0:T(8,128)(2,1)S(1)} collective-permute-done((bf16[32,2,16,128]{3,2,1,0:T(8,128)(2,1)S(1)}, bf16[32,2,16,128]{3,2,1,0:T(8,128)(2,1)S(1)}, u32[]{:S(2)}, u32[]{:S(2)}) %collective-permute-start) | collective-permute-done | bytes 262176 | tf_op jit(solution)/shard_map/ppermute | solution.py:213
  39.2 1.4 %collective-permute-start.5 = (bf16[32,2,16,128]{3,2,1,0:T(8,128)(2,1)S(1)}, bf16[32,2,16,128]{3,2,1,0:T(8,128)(2,1)S(1)}, u32[]{:S(2)}, u32[]{:S(2)}) collective-permute-start(bf16[32,2,16,128]{3,2,1,0:T(8,128)(2,1)S(1)} %collective-permute-done.refs_1_), channel_id=1, source_target_pairs={{0,1},{1,0},{2,3},{3,2},{4,5},{5,4},{6,7},{7,6},{8,9},{9,8},{10,11... | collective-permute-start | bytes 786440 | tf_op jit(solution)/shard_map/ppermute | solution.py:217
  40.6 5.1 %collective-permute-start.1 = (bf16[32,2,16,128]{3,2,1,0:T(8,128)(2,1)S(1)}, bf16[32,2,16,128]{3,2,1,0:T(8,128)(2,1)S(1)}, u32[]{:S(2)}, u32[]{:S(2)}) collective-permute-start(bf16[32,2,16,128]{3,2,1,0:T(8,128)(2,1)S(1)} %collective-permute-done.refs_1_), channel_id=1, source_target_pairs={{0,2},{1,7},{2,4},{3,1},{4,6},{5,3},{6,0},{7,5},{8,10},{9,15},{10,... | collective-permute-start | bytes 786440 | tf_op jit(solution)/shard_map/ppermute | solution.py:213
  45.6 1.3 %collective-permute-done.3.refs_3_ = bf16[32,2,16,128]{3,2,1,0:T(8,128)(2,1)S(1)} collective-permute-done((bf16[32,2,16,128]{3,2,1,0:T(8,128)(2,1)S(1)}, bf16[32,2,16,128]{3,2,1,0:T(8,128)(2,1)S(1)}, u32[]{:S(2)}, u32[]{:S(2)}) %collective-permute-start.3) | collective-permute-done | bytes 262176 | tf_op jit(solution)/shard_map/ppermute | solution.py:213
  47.0 0.0 collective-permute-start.4
  47.0 0.0 collective-permute-done.5.refs_2_
  47.0 2.0 %shard_map.39.refs_3_ = bf16[2,512,4096]{2,1,0:T(8,128)(2,1)} custom-call(bf16[32,2,16,128]{3,2,1,0:T(8,128)(2,1)S(1)} %bitcast.8, bf16[32,2,16,128]{3,2,1,0:T(8,128)(2,1)S(1)} %collective-permute-done.refs_1_, bf16[32,2,16,128]{3,2,1,0:T(8,128)(2,1)S(1)} %collective-permute-done.5.refs_2_, ...), custom_call_target="tpu_custom_call", output_to_operand_aliasing={{}: (4, {})} | custom-call | flops 1 | bytes 1 | tf_op jit(solution)/shard_map/pallas_call | solution.py:196
  49.0 1.0 %collective-permute-done.1.refs_2_ = bf16[32,2,16,128]{3,2,1,0:T(8,128)(2,1)S(1)} collective-permute-done((bf16[32,2,16,128]{3,2,1,0:T(8,128)(2,1)S(1)}, bf16[32,2,16,128]{3,2,1,0:T(8,128)(2,1)S(1)}, u32[]{:S(2)}, u32[]{:S(2)}) %collective-permute-start.1) | collective-permute-done | bytes 262176 | tf_op jit(solution)/shard_map/ppermute | solution.py:213
  49.9 0.0 collective-permute-done.4.refs_1_
  49.9 2.5 %collective-permute-start.6 = (bf16[32,2,16,128]{3,2,1,0:T(8,128)(2,1)S(1)}, bf16[32,2,16,128]{3,2,1,0:T(8,128)(2,1)S(1)}, u32[]{:S(2)}, u32[]{:S(2)}) collective-permute-start(bf16[32,2,16,128]{3,2,1,0:T(8,128)(2,1)S(1)} %collective-permute-done.1.refs_2_), channel_id=1, source_target_pairs={{0,1},{1,0},{2,3},{3,2},{4,5},{5,4},{6,7},{7,6},{8,9},{9,8},{10,11... | collective-permute-start | bytes 786440 | tf_op jit(solution)/shard_map/ppermute | solution.py:217
  52.4 1.6 %shard_map.40.refs_2_ = bf16[2,512,4096]{2,1,0:T(8,128)(2,1)} custom-call(bf16[32,2,16,128]{3,2,1,0:T(8,128)(2,1)S(1)} %bitcast.9, bf16[32,2,16,128]{3,2,1,0:T(8,128)(2,1)S(1)} %collective-permute-done.4.refs_1_, bf16[32,2,16,128]{3,2,1,0:T(8,128)(2,1)S(1)} %collective-permute-done.1.refs_2_, ...), custom_call_target="tpu_custom_call", output_to_operand_aliasing={{}: (3, {})} | custom-call | flops 1 | bytes 1 | tf_op jit(solution)/shard_map/pallas_call | solution.py:196
  54.1 0.0 collective-permute-done.6.refs_1_
  54.1 1.3 %shard_map.41 = bf16[2,512,4096]{2,1,0:T(8,128)(2,1)} custom-call(bf16[32,2,16,128]{3,2,1,0:T(8,128)(2,1)S(1)} %bitcast.10, bf16[32,2,16,128]{3,2,1,0:T(8,128)(2,1)S(1)} %collective-permute-done.6.refs_1_, bf16[2,512,4096]{2,1,0:T(8,128)(2,1)} %shard_map.40.refs_2_), custom_call_target="tpu_custom_call", output_to_operand_aliasing={{}: (2, {})} | custom-call | flops 1 | bytes 1 | tf_op jit(solution)/shard_map/pallas_call | solution.py:196
Async XLA Ops:
  25.9 6.9 %collective-permute-start.2 = (bf16[32,2,16,128]{3,2,1,0:T(8,128)(2,1)S(1)}, bf16[32,2,16,128]{3,2,1,0:T(8,128)(2,1)S(1)}, u32[]{:S(2)}, u32[]{:S(2)}) collective-permute-start(bf16[32,2,16,128]{3,2,1,0:T(8,128)(2,1)S(1)} %bitcast.4), channel_id=1, source_target_pairs={{0,1},{1,0},{2,3},{3,2},{4,5},{5,4},{6,7},{7,6},{8,9},{9,8},{10,11... | collective-permute-start | bytes 786440 | tf_op jit(solution)/shard_map/ppermute | solution.py:217
  27.7 11.4 %collective-permute-start = (bf16[32,2,16,128]{3,2,1,0:T(8,128)(2,1)S(1)}, bf16[32,2,16,128]{3,2,1,0:T(8,128)(2,1)S(1)}, u32[]{:S(2)}, u32[]{:S(2)}) collective-permute-start(bf16[32,2,16,128]{3,2,1,0:T(8,128)(2,1)S(1)} %bitcast.5), channel_id=1, source_target_pairs={{0,2},{1,7},{2,4},{3,1},{4,6},{5,3},{6,0},{7,5},{8,10},{9,15},{10,... | collective-permute-start | bytes 786440 | tf_op jit(solution)/shard_map/ppermute | solution.py:213
  34.5 12.4 %collective-permute-start.3 = (bf16[32,2,16,128]{3,2,1,0:T(8,128)(2,1)S(1)}, bf16[32,2,16,128]{3,2,1,0:T(8,128)(2,1)S(1)}, u32[]{:S(2)}, u32[]{:S(2)}) collective-permute-start(bf16[32,2,16,128]{3,2,1,0:T(8,128)(2,1)S(1)} %collective-permute-done.2.refs_2_), channel_id=1, source_target_pairs={{0,2},{1,7},{2,4},{3,1},{4,6},{5,3},{6,0},{7,5},{8,10},{9,15},{10,... | collective-permute-start | bytes 786440 | tf_op jit(solution)/shard_map/ppermute | solution.py:213
  39.2 7.8 %collective-permute-start.5 = (bf16[32,2,16,128]{3,2,1,0:T(8,128)(2,1)S(1)}, bf16[32,2,16,128]{3,2,1,0:T(8,128)(2,1)S(1)}, u32[]{:S(2)}, u32[]{:S(2)}) collective-permute-start(bf16[32,2,16,128]{3,2,1,0:T(8,128)(2,1)S(1)} %collective-permute-done.refs_1_), channel_id=1, source_target_pairs={{0,1},{1,0},{2,3},{3,2},{4,5},{5,4},{6,7},{7,6},{8,9},{9,8},{10,11... | collective-permute-start | bytes 786440 | tf_op jit(solution)/shard_map/ppermute | solution.py:217
  40.6 9.4 %collective-permute-start.1 = (bf16[32,2,16,128]{3,2,1,0:T(8,128)(2,1)S(1)}, bf16[32,2,16,128]{3,2,1,0:T(8,128)(2,1)S(1)}, u32[]{:S(2)}, u32[]{:S(2)}) collective-permute-start(bf16[32,2,16,128]{3,2,1,0:T(8,128)(2,1)S(1)} %collective-permute-done.refs_1_), channel_id=1, source_target_pairs={{0,2},{1,7},{2,4},{3,1},{4,6},{5,3},{6,0},{7,5},{8,10},{9,15},{10,... | collective-permute-start | bytes 786440 | tf_op jit(solution)/shard_map/ppermute | solution.py:213
  47.0 3.0 %collective-permute-start.4 = (bf16[32,2,16,128]{3,2,1,0:T(8,128)(2,1)S(1)}, bf16[32,2,16,128]{3,2,1,0:T(8,128)(2,1)S(1)}, u32[]{:S(2)}, u32[]{:S(2)}) collective-permute-start(bf16[32,2,16,128]{3,2,1,0:T(8,128)(2,1)S(1)} %collective-permute-done.3.refs_3_), channel_id=1, source_target_pairs={{0,1},{1,0},{2,3},{3,2},{4,5},{5,4},{6,7},{7,6},{8,9},{9,8},{10,11... | collective-permute-start | bytes 786440 | tf_op jit(solution)/shard_map/ppermute | solution.py:217
  49.9 4.1 %collective-permute-start.6 = (bf16[32,2,16,128]{3,2,1,0:T(8,128)(2,1)S(1)}, bf16[32,2,16,128]{3,2,1,0:T(8,128)(2,1)S(1)}, u32[]{:S(2)}, u32[]{:S(2)}) collective-permute-start(bf16[32,2,16,128]{3,2,1,0:T(8,128)(2,1)S(1)} %collective-permute-done.1.refs_2_), channel_id=1, source_target_pairs={{0,1},{1,0},{2,3},{3,2},{4,5},{5,4},{6,7},{7,6},{8,9},{9,8},{10,11... | collective-permute-start | bytes 786440 | tf_op jit(solution)/shard_map/ppermute | solution.py:217

commit v5 on v4

--- a/solution.py
+++ b/solution.py
@@ -131,7 +131,7 @@
 
     lax.fori_loop(0, tiles, column, 0)
     table_copy.wait()
-    product[...] = jnp.dot(filtered[...], table[...], preferred_element_type=jnp.float32)
+    product[: FRAMES * INPUTS_HERE, :] = jnp.dot(filtered[...], table[...], preferred_element_type=jnp.float32)
     for i in range(INPUTS_HERE):
         turned[i * LANES : (i + 1) * LANES, :] = product[
             pl.ds(i, FRAMES, stride=INPUTS_HERE), :
@@ -156,8 +156,8 @@
             pltpu.VMEM((TAPS, FRAME_LEN), jnp.float32),
             pltpu.VMEM((FRAME_LEN, 2 * CHANNELS), jnp.bfloat16),
             pltpu.VMEM((FRAMES * INPUTS_HERE, FRAME_LEN), jnp.bfloat16),
-            pltpu.VMEM((FRAMES * INPUTS_HERE, 2 * CHANNELS), jnp.float32),
-            pltpu.VMEM((FRAMES * INPUTS_HERE, FRAMES), jnp.float32),
+            pltpu.VMEM(((FRAMES + 1) * INPUTS_HERE, 2 * CHANNELS), jnp.float32),
+            pltpu.VMEM(((ROWS + 1) * CHANNELS, FRAMES), jnp.float32),
             pltpu.SemaphoreType.DMA((FRAME_LEN // LANES + 2,)),
         ],
         compiler_params=pltpu.CompilerParams(vmem_limit_bytes=VMEM_LIMIT),

time: 55.5 us -> 55.6 us (level)
  no operation moved by 1% of the time
where the time goes in v5:
time: 55.6 us; the launch traced here: 55.4 us
  Pallas kernels  17.1 us (31%)
  starting transfers between devices  17.1 us (31%)
  blocking collectives  15.5 us (28%)
  waiting for transfers between devices  5.69 us (10%)
    all_to_all x1, blocking collectives, shards(): lax.all_to_all(spectra, ('z_lo', 'x', 'y'), split_axis=0, concat_axis=0,...  15.5 us
    ppermute x3, starting transfers between devices, onward(): return lax.ppermute(block, ('z_hi', 'core'), way)  11.4 us
    pallas_call x1, Pallas kernels, channelize(): pl.pallas_call(channelize_kernel, out_shape=jax.ShapeDtypeStruct((CHANNEL...  10.5 us
    pallas_call x4, Pallas kernels, correlate(): pl.pallas_call(functools.partial(correlate_kernel, places, 0 if held is N...  6.58 us
    ppermute x3, waiting for transfers between devices, onward(): return lax.ppermute(block, ('z_hi', 'core'), way)  5.68 us
    ppermute x4, starting transfers between devices, swap(): return lax.ppermute(block, 'core', [(0, 1), (1, 0)])  5.68 us
  transfers between devices with their start and end apart: 7, of which 3 were waited for; matrix products, arithmetic and copies ran while one was open for 0% of the time, Pallas kernels for 10%

profile of v5, /device:TPU:33, one launch (start us, length us, event | category | flops | bytes accessed | tf_op | source)
XLA Modules:
  0.0 55.4 jit_solution(7765693315276818092)
XLA Ops:
  0.0 10.5 %shard_map.37 = bf16[64,16,128]{2,1,0:T(8,128)(2,1)} custom-call(bf16[143,8,2048]{2,1,0:T(8,128)(2,1)} %bitcast.11, f32[16,2048]{1,0:T(8,128)} %taps_hbm.1, bf16[2048,128]{1,0:T(8,128)(2,1)} %constant.2.clone.table_hbm), custom_call_target="tpu_custom_call" | custom-call | tf_op jit(solution)/shard_map/pallas_call | solution.py:149
  10.5 15.5 %all_to_all.5 = bf16[64,16,128]{2,1,0:T(8,128)(2,1)S(1)} all-to-all(bf16[64,16,128]{2,1,0:T(8,128)(2,1)} %shard_map.37), channel_id=1, replica_groups=mesh['z_lo'=2,'x'=4,'y'=4,'z_hi'=4,'core'=2] {'z_lo','x','y'}, dimensions={0} | all-to-all | bytes 524288 | tf_op jit(solution)/shard_map/all_to_all | solution.py:222
  26.0 1.8 %collective-permute-start.2 = (bf16[32,2,16,128]{3,2,1,0:T(8,128)(2,1)S(1)}, bf16[32,2,16,128]{3,2,1,0:T(8,128)(2,1)S(1)}, u32[]{:S(2)}, u32[]{:S(2)}) collective-permute-start(bf16[32,2,16,128]{3,2,1,0:T(8,128)(2,1)S(1)} %bitcast.4), channel_id=1, source_target_pairs={{0,1},{1,0},{2,3},{3,2},{4,5},{5,4},{6,7},{7,6},{8,9},{9,8},{10,11... | collective-permute-start | bytes 786440 | tf_op jit(solution)/shard_map/ppermute | solution.py:217
  27.8 5.1 %collective-permute-start = (bf16[32,2,16,128]{3,2,1,0:T(8,128)(2,1)S(1)}, bf16[32,2,16,128]{3,2,1,0:T(8,128)(2,1)S(1)}, u32[]{:S(2)}, u32[]{:S(2)}) collective-permute-start(bf16[32,2,16,128]{3,2,1,0:T(8,128)(2,1)S(1)} %bitcast.5), channel_id=1, source_target_pairs={{0,2},{1,7},{2,4},{3,1},{4,6},{5,3},{6,0},{7,5},{8,10},{9,15},{10,... | collective-permute-start | bytes 786440 | tf_op jit(solution)/shard_map/ppermute | solution.py:213
  32.9 0.0 collective-permute-done.2.refs_2_
  32.9 1.6 %shard_map.38.refs_4_ = bf16[2,512,4096]{2,1,0:T(8,128)(2,1)} custom-call(bf16[32,2,16,128]{3,2,1,0:T(8,128)(2,1)S(1)} %bitcast.6, bf16[32,2,16,128]{3,2,1,0:T(8,128)(2,1)S(1)} %bitcast.7, bf16[32,2,16,128]{3,2,1,0:T(8,128)(2,1)S(1)} %collective-permute-done.2.refs_2_), custom_call_target="tpu_custom_call" | custom-call | flops 1 | bytes 1 | tf_op jit(solution)/shard_map/pallas_call | solution.py:196
  34.6 1.2 %collective-permute-start.3 = (bf16[32,2,16,128]{3,2,1,0:T(8,128)(2,1)S(1)}, bf16[32,2,16,128]{3,2,1,0:T(8,128)(2,1)S(1)}, u32[]{:S(2)}, u32[]{:S(2)}) collective-permute-start(bf16[32,2,16,128]{3,2,1,0:T(8,128)(2,1)S(1)} %collective-permute-done.2.refs_2_), channel_id=1, source_target_pairs={{0,2},{1,7},{2,4},{3,1},{4,6},{5,3},{6,0},{7,5},{8,10},{9,15},{10,... | collective-permute-start | bytes 786440 | tf_op jit(solution)/shard_map/ppermute | solution.py:213
  35.8 3.4 %collective-permute-done.refs_1_ = bf16[32,2,16,128]{3,2,1,0:T(8,128)(2,1)S(1)} collective-permute-done((bf16[32,2,16,128]{3,2,1,0:T(8,128)(2,1)S(1)}, bf16[32,2,16,128]{3,2,1,0:T(8,128)(2,1)S(1)}, u32[]{:S(2)}, u32[]{:S(2)}) %collective-permute-start) | collective-permute-done | bytes 262176 | tf_op jit(solution)/shard_map/ppermute | solution.py:213
  39.2 1.4 %collective-permute-start.5 = (bf16[32,2,16,128]{3,2,1,0:T(8,128)(2,1)S(1)}, bf16[32,2,16,128]{3,2,1,0:T(8,128)(2,1)S(1)}, u32[]{:S(2)}, u32[]{:S(2)}) collective-permute-start(bf16[32,2,16,128]{3,2,1,0:T(8,128)(2,1)S(1)} %collective-permute-done.refs_1_), channel_id=1, source_target_pairs={{0,1},{1,0},{2,3},{3,2},{4,5},{5,4},{6,7},{7,6},{8,9},{9,8},{10,11... | collective-permute-start | bytes 786440 | tf_op jit(solution)/shard_map/ppermute | solution.py:217
  40.6 5.1 %collective-permute-start.1 = (bf16[32,2,16,128]{3,2,1,0:T(8,128)(2,1)S(1)}, bf16[32,2,16,128]{3,2,1,0:T(8,128)(2,1)S(1)}, u32[]{:S(2)}, u32[]{:S(2)}) collective-permute-start(bf16[32,2,16,128]{3,2,1,0:T(8,128)(2,1)S(1)} %collective-permute-done.refs_1_), channel_id=1, source_target_pairs={{0,2},{1,7},{2,4},{3,1},{4,6},{5,3},{6,0},{7,5},{8,10},{9,15},{10,... | collective-permute-start | bytes 786440 | tf_op jit(solution)/shard_map/ppermute | solution.py:213
  45.7 1.3 %collective-permute-done.3.refs_3_ = bf16[32,2,16,128]{3,2,1,0:T(8,128)(2,1)S(1)} collective-permute-done((bf16[32,2,16,128]{3,2,1,0:T(8,128)(2,1)S(1)}, bf16[32,2,16,128]{3,2,1,0:T(8,128)(2,1)S(1)}, u32[]{:S(2)}, u32[]{:S(2)}) %collective-permute-start.3) | collective-permute-done | bytes 262176 | tf_op jit(solution)/shard_map/ppermute | solution.py:213
  47.0 0.0 collective-permute-start.4
  47.0 0.0 collective-permute-done.5.refs_2_
  47.0 2.0 %shard_map.39.refs_3_ = bf16[2,512,4096]{2,1,0:T(8,128)(2,1)} custom-call(bf16[32,2,16,128]{3,2,1,0:T(8,128)(2,1)S(1)} %bitcast.8, bf16[32,2,16,128]{3,2,1,0:T(8,128)(2,1)S(1)} %collective-permute-done.refs_1_, bf16[32,2,16,128]{3,2,1,0:T(8,128)(2,1)S(1)} %collective-permute-done.5.refs_2_, ...), custom_call_target="tpu_custom_call", output_to_operand_aliasing={{}: (4, {})} | custom-call | flops 1 | bytes 1 | tf_op jit(solution)/shard_map/pallas_call | solution.py:196
  49.0 1.0 %collective-permute-done.1.refs_2_ = bf16[32,2,16,128]{3,2,1,0:T(8,128)(2,1)S(1)} collective-permute-done((bf16[32,2,16,128]{3,2,1,0:T(8,128)(2,1)S(1)}, bf16[32,2,16,128]{3,2,1,0:T(8,128)(2,1)S(1)}, u32[]{:S(2)}, u32[]{:S(2)}) %collective-permute-start.1) | collective-permute-done | bytes 262176 | tf_op jit(solution)/shard_map/ppermute | solution.py:213
  50.0 0.0 collective-permute-done.4.refs_1_
  50.0 2.5 %collective-permute-start.6 = (bf16[32,2,16,128]{3,2,1,0:T(8,128)(2,1)S(1)}, bf16[32,2,16,128]{3,2,1,0:T(8,128)(2,1)S(1)}, u32[]{:S(2)}, u32[]{:S(2)}) collective-permute-start(bf16[32,2,16,128]{3,2,1,0:T(8,128)(2,1)S(1)} %collective-permute-done.1.refs_2_), channel_id=1, source_target_pairs={{0,1},{1,0},{2,3},{3,2},{4,5},{5,4},{6,7},{7,6},{8,9},{9,8},{10,11... | collective-permute-start | bytes 786440 | tf_op jit(solution)/shard_map/ppermute | solution.py:217
  52.5 1.6 %shard_map.40.refs_2_ = bf16[2,512,4096]{2,1,0:T(8,128)(2,1)} custom-call(bf16[32,2,16,128]{3,2,1,0:T(8,128)(2,1)S(1)} %bitcast.9, bf16[32,2,16,128]{3,2,1,0:T(8,128)(2,1)S(1)} %collective-permute-done.4.refs_1_, bf16[32,2,16,128]{3,2,1,0:T(8,128)(2,1)S(1)} %collective-permute-done.1.refs_2_, ...), custom_call_target="tpu_custom_call", output_to_operand_aliasing={{}: (3, {})} | custom-call | flops 1 | bytes 1 | tf_op jit(solution)/shard_map/pallas_call | solution.py:196
  54.1 0.0 collective-permute-done.6.refs_1_
  54.1 1.3 %shard_map.41 = bf16[2,512,4096]{2,1,0:T(8,128)(2,1)} custom-call(bf16[32,2,16,128]{3,2,1,0:T(8,128)(2,1)S(1)} %bitcast.10, bf16[32,2,16,128]{3,2,1,0:T(8,128)(2,1)S(1)} %collective-permute-done.6.refs_1_, bf16[2,512,4096]{2,1,0:T(8,128)(2,1)} %shard_map.40.refs_2_), custom_call_target="tpu_custom_call", output_to_operand_aliasing={{}: (2, {})} | custom-call | flops 1 | bytes 1 | tf_op jit(solution)/shard_map/pallas_call | solution.py:196
Async XLA Ops:
  26.0 6.9 %collective-permute-start.2 = (bf16[32,2,16,128]{3,2,1,0:T(8,128)(2,1)S(1)}, bf16[32,2,16,128]{3,2,1,0:T(8,128)(2,1)S(1)}, u32[]{:S(2)}, u32[]{:S(2)}) collective-permute-start(bf16[32,2,16,128]{3,2,1,0:T(8,128)(2,1)S(1)} %bitcast.4), channel_id=1, source_target_pairs={{0,1},{1,0},{2,3},{3,2},{4,5},{5,4},{6,7},{7,6},{8,9},{9,8},{10,11... | collective-permute-start | bytes 786440 | tf_op jit(solution)/shard_map/ppermute | solution.py:217
  27.8 11.4 %collective-permute-start = (bf16[32,2,16,128]{3,2,1,0:T(8,128)(2,1)S(1)}, bf16[32,2,16,128]{3,2,1,0:T(8,128)(2,1)S(1)}, u32[]{:S(2)}, u32[]{:S(2)}) collective-permute-start(bf16[32,2,16,128]{3,2,1,0:T(8,128)(2,1)S(1)} %bitcast.5), channel_id=1, source_target_pairs={{0,2},{1,7},{2,4},{3,1},{4,6},{5,3},{6,0},{7,5},{8,10},{9,15},{10,... | collective-permute-start | bytes 786440 | tf_op jit(solution)/shard_map/ppermute | solution.py:213
  34.6 12.4 %collective-permute-start.3 = (bf16[32,2,16,128]{3,2,1,0:T(8,128)(2,1)S(1)}, bf16[32,2,16,128]{3,2,1,0:T(8,128)(2,1)S(1)}, u32[]{:S(2)}, u32[]{:S(2)}) collective-permute-start(bf16[32,2,16,128]{3,2,1,0:T(8,128)(2,1)S(1)} %collective-permute-done.2.refs_2_), channel_id=1, source_target_pairs={{0,2},{1,7},{2,4},{3,1},{4,6},{5,3},{6,0},{7,5},{8,10},{9,15},{10,... | collective-permute-start | bytes 786440 | tf_op jit(solution)/shard_map/ppermute | solution.py:213
  39.2 7.8 %collective-permute-start.5 = (bf16[32,2,16,128]{3,2,1,0:T(8,128)(2,1)S(1)}, bf16[32,2,16,128]{3,2,1,0:T(8,128)(2,1)S(1)}, u32[]{:S(2)}, u32[]{:S(2)}) collective-permute-start(bf16[32,2,16,128]{3,2,1,0:T(8,128)(2,1)S(1)} %collective-permute-done.refs_1_), channel_id=1, source_target_pairs={{0,1},{1,0},{2,3},{3,2},{4,5},{5,4},{6,7},{7,6},{8,9},{9,8},{10,11... | collective-permute-start | bytes 786440 | tf_op jit(solution)/shard_map/ppermute | solution.py:217
  40.6 9.4 %collective-permute-start.1 = (bf16[32,2,16,128]{3,2,1,0:T(8,128)(2,1)S(1)}, bf16[32,2,16,128]{3,2,1,0:T(8,128)(2,1)S(1)}, u32[]{:S(2)}, u32[]{:S(2)}) collective-permute-start(bf16[32,2,16,128]{3,2,1,0:T(8,128)(2,1)S(1)} %collective-permute-done.refs_1_), channel_id=1, source_target_pairs={{0,2},{1,7},{2,4},{3,1},{4,6},{5,3},{6,0},{7,5},{8,10},{9,15},{10,... | collective-permute-start | bytes 786440 | tf_op jit(solution)/shard_map/ppermute | solution.py:213
  47.0 3.0 %collective-permute-start.4 = (bf16[32,2,16,128]{3,2,1,0:T(8,128)(2,1)S(1)}, bf16[32,2,16,128]{3,2,1,0:T(8,128)(2,1)S(1)}, u32[]{:S(2)}, u32[]{:S(2)}) collective-permute-start(bf16[32,2,16,128]{3,2,1,0:T(8,128)(2,1)S(1)} %collective-permute-done.3.refs_3_), channel_id=1, source_target_pairs={{0,1},{1,0},{2,3},{3,2},{4,5},{5,4},{6,7},{7,6},{8,9},{9,8},{10,11... | collective-permute-start | bytes 786440 | tf_op jit(solution)/shard_map/ppermute | solution.py:217
  50.0 4.1 %collective-permute-start.6 = (bf16[32,2,16,128]{3,2,1,0:T(8,128)(2,1)S(1)}, bf16[32,2,16,128]{3,2,1,0:T(8,128)(2,1)S(1)}, u32[]{:S(2)}, u32[]{:S(2)}) collective-permute-start(bf16[32,2,16,128]{3,2,1,0:T(8,128)(2,1)S(1)} %collective-permute-done.1.refs_2_), channel_id=1, source_target_pairs={{0,1},{1,0},{2,3},{3,2},{4,5},{5,4},{6,7},{7,6},{8,9},{9,8},{10,11... | collective-permute-start | bytes 786440 | tf_op jit(solution)/shard_map/ppermute | solution.py:217

commit v6 on v5

--- a/solution.py
+++ b/solution.py
@@ -24,6 +24,7 @@
 ROWS = 2 * INPUTS_HERE
 STRIP_ROWS = PEERS * ROWS
 STRIPS = 8
+PARTS = 2
 VMEM_LIMIT = 60 * 2**20
 CORRELATE_LIMIT = 16 * 2**20
 
@@ -177,14 +178,21 @@
         for ch in range(OWN):
             left = left_ref[:, ch].reshape(STRIP_ROWS, FRAMES)
             right = block[:, ch].reshape(STRIP_ROWS, FRAMES)
-            got = lax.dot_general(
-                left, right, (((1,), (1,)), ((), ())), preferred_element_type=jnp.float32
-            )
-            slot = len(writes)
-            stage[slot] = (got * (1.0 / FRAMES)).astype(jnp.bfloat16)
-            write = pltpu.make_async_copy(stage.at[slot], out_hbm.at[ch, :, span], sems.at[slot])
-            write.start()
-            writes.append(write)
+            for part in range(PARTS):
+                slot = len(writes)
+                rows = slice(part * STRIP_ROWS // PARTS, (part + 1) * STRIP_ROWS // PARTS)
+                got = lax.dot_general(
+                    left[rows],
+                    right,
+                    (((1,), (1,)), ((), ())),
+                    preferred_element_type=jnp.float32,
+                )
+                stage[slot] = (got * (1.0 / FRAMES)).astype(jnp.bfloat16)
+                write = pltpu.make_async_copy(
+                    stage.at[slot], out_hbm.at[ch, rows, span], sems.at[slot]
+                )
+                write.start()
+                writes.append(write)
     for write in writes:
         write.wait()
 
@@ -199,8 +207,8 @@
         in_specs=[pl.BlockSpec(memory_space=space) for space in spaces],
         out_specs=pl.BlockSpec(memory_space=pl.ANY),
         scratch_shapes=[
-            pltpu.VMEM((OWN * count, STRIP_ROWS, STRIP_ROWS), jnp.bfloat16),
-            pltpu.SemaphoreType.DMA((OWN * count,)),
+            pltpu.VMEM((OWN * count * PARTS, STRIP_ROWS // PARTS, STRIP_ROWS), jnp.bfloat16),
+            pltpu.SemaphoreType.DMA((OWN * count * PARTS,)),
         ],
         input_output_aliases={} if held is None else {count + 1: 0},
         cost_estimate=pl.CostEstimate(flops=1, bytes_accessed=1, transcendentals=0),

time: 55.6 us -> 55.5 us (level)
  transfers between devices with their start and end apart: 7 -> 7, of which waited for: 3 -> 3; matrix products, arithmetic and copies ran while one was open for 0% -> 0% of each run, Pallas kernels for 10% -> 9%
where the time goes in v6:
time: 55.5 us; the launch traced here: 55.3 us
  starting transfers between devices  17.1 us (31%)
  Pallas kernels  16.9 us (30%)
  blocking collectives  15.5 us (28%)
  waiting for transfers between devices  5.76 us (10%)
    all_to_all x1, blocking collectives, shards(): lax.all_to_all(spectra, ('z_lo', 'x', 'y'), split_axis=0, concat_axis=0,...  15.5 us
    ppermute x3, starting transfers between devices, onward(): return lax.ppermute(block, ('z_hi', 'core'), way)  11.4 us
    pallas_call x1, Pallas kernels, channelize(): pl.pallas_call(channelize_kernel, out_shape=jax.ShapeDtypeStruct((CHANNEL...  10.5 us
    pallas_call x4, Pallas kernels, correlate(): pl.pallas_call(functools.partial(correlate_kernel, places, 0 if held is N...  6.43 us
    ppermute x3, waiting for transfers between devices, onward(): return lax.ppermute(block, ('z_hi', 'core'), way)  5.74 us
    ppermute x4, starting transfers between devices, swap(): return lax.ppermute(block, 'core', [(0, 1), (1, 0)])  5.68 us
  transfers between devices with their start and end apart: 7, of which 3 were waited for; matrix products, arithmetic and copies ran while one was open for 0% of the time, Pallas kernels for 9%

profile of v6, /device:TPU:33, one launch (start us, length us, event | category | flops | bytes accessed | tf_op | source)
XLA Modules:
  0.0 55.3 jit_solution(15256125752870984021)
XLA Ops:
  0.0 10.5 %shard_map.37 = bf16[64,16,128]{2,1,0:T(8,128)(2,1)} custom-call(bf16[143,8,2048]{2,1,0:T(8,128)(2,1)} %bitcast.11, f32[16,2048]{1,0:T(8,128)} %taps_hbm.1, bf16[2048,128]{1,0:T(8,128)(2,1)} %constant.2.clone.table_hbm), custom_call_target="tpu_custom_call" | custom-call | tf_op jit(solution)/shard_map/pallas_call | solution.py:150
  10.5 15.5 %all_to_all.5 = bf16[64,16,128]{2,1,0:T(8,128)(2,1)S(1)} all-to-all(bf16[64,16,128]{2,1,0:T(8,128)(2,1)} %shard_map.37), channel_id=1, replica_groups=mesh['z_lo'=2,'x'=4,'y'=4,'z_hi'=4,'core'=2] {'z_lo','x','y'}, dimensions={0} | all-to-all | bytes 524288 | tf_op jit(solution)/shard_map/all_to_all | solution.py:230
  26.0 1.8 %collective-permute-start.2 = (bf16[32,2,16,128]{3,2,1,0:T(8,128)(2,1)S(1)}, bf16[32,2,16,128]{3,2,1,0:T(8,128)(2,1)S(1)}, u32[]{:S(2)}, u32[]{:S(2)}) collective-permute-start(bf16[32,2,16,128]{3,2,1,0:T(8,128)(2,1)S(1)} %bitcast.4), channel_id=1, source_target_pairs={{0,1},{1,0},{2,3},{3,2},{4,5},{5,4},{6,7},{7,6},{8,9},{9,8},{10,11... | collective-permute-start | bytes 786440 | tf_op jit(solution)/shard_map/ppermute | solution.py:225
  27.8 5.1 %collective-permute-start = (bf16[32,2,16,128]{3,2,1,0:T(8,128)(2,1)S(1)}, bf16[32,2,16,128]{3,2,1,0:T(8,128)(2,1)S(1)}, u32[]{:S(2)}, u32[]{:S(2)}) collective-permute-start(bf16[32,2,16,128]{3,2,1,0:T(8,128)(2,1)S(1)} %bitcast.5), channel_id=1, source_target_pairs={{0,2},{1,7},{2,4},{3,1},{4,6},{5,3},{6,0},{7,5},{8,10},{9,15},{10,... | collective-permute-start | bytes 786440 | tf_op jit(solution)/shard_map/ppermute | solution.py:221
  32.9 0.0 collective-permute-done.2.refs_2_
  32.9 1.6 %shard_map.38.refs_4_ = bf16[2,512,4096]{2,1,0:T(8,128)(2,1)} custom-call(bf16[32,2,16,128]{3,2,1,0:T(8,128)(2,1)S(1)} %bitcast.6, bf16[32,2,16,128]{3,2,1,0:T(8,128)(2,1)S(1)} %bitcast.7, bf16[32,2,16,128]{3,2,1,0:T(8,128)(2,1)S(1)} %collective-permute-done.2.refs_2_), custom_call_target="tpu_custom_call" | custom-call | flops 1 | bytes 1 | tf_op jit(solution)/shard_map/pallas_call | solution.py:204
  34.6 1.2 %collective-permute-start.3 = (bf16[32,2,16,128]{3,2,1,0:T(8,128)(2,1)S(1)}, bf16[32,2,16,128]{3,2,1,0:T(8,128)(2,1)S(1)}, u32[]{:S(2)}, u32[]{:S(2)}) collective-permute-start(bf16[32,2,16,128]{3,2,1,0:T(8,128)(2,1)S(1)} %collective-permute-done.2.refs_2_), channel_id=1, source_target_pairs={{0,2},{1,7},{2,4},{3,1},{4,6},{5,3},{6,0},{7,5},{8,10},{9,15},{10,... | collective-permute-start | bytes 786440 | tf_op jit(solution)/shard_map/ppermute | solution.py:221
  35.8 3.4 %collective-permute-done.refs_1_ = bf16[32,2,16,128]{3,2,1,0:T(8,128)(2,1)S(1)} collective-permute-done((bf16[32,2,16,128]{3,2,1,0:T(8,128)(2,1)S(1)}, bf16[32,2,16,128]{3,2,1,0:T(8,128)(2,1)S(1)}, u32[]{:S(2)}, u32[]{:S(2)}) %collective-permute-start) | collective-permute-done | bytes 262176 | tf_op jit(solution)/shard_map/ppermute | solution.py:221
  39.2 1.4 %collective-permute-start.5 = (bf16[32,2,16,128]{3,2,1,0:T(8,128)(2,1)S(1)}, bf16[32,2,16,128]{3,2,1,0:T(8,128)(2,1)S(1)}, u32[]{:S(2)}, u32[]{:S(2)}) collective-permute-start(bf16[32,2,16,128]{3,2,1,0:T(8,128)(2,1)S(1)} %collective-permute-done.refs_1_), channel_id=1, source_target_pairs={{0,1},{1,0},{2,3},{3,2},{4,5},{5,4},{6,7},{7,6},{8,9},{9,8},{10,11... | collective-permute-start | bytes 786440 | tf_op jit(solution)/shard_map/ppermute | solution.py:225
  40.7 5.0 %collective-permute-start.1 = (bf16[32,2,16,128]{3,2,1,0:T(8,128)(2,1)S(1)}, bf16[32,2,16,128]{3,2,1,0:T(8,128)(2,1)S(1)}, u32[]{:S(2)}, u32[]{:S(2)}) collective-permute-start(bf16[32,2,16,128]{3,2,1,0:T(8,128)(2,1)S(1)} %collective-permute-done.refs_1_), channel_id=1, source_target_pairs={{0,2},{1,7},{2,4},{3,1},{4,6},{5,3},{6,0},{7,5},{8,10},{9,15},{10,... | collective-permute-start | bytes 786440 | tf_op jit(solution)/shard_map/ppermute | solution.py:221
  45.7 1.3 %collective-permute-done.3.refs_3_ = bf16[32,2,16,128]{3,2,1,0:T(8,128)(2,1)S(1)} collective-permute-done((bf16[32,2,16,128]{3,2,1,0:T(8,128)(2,1)S(1)}, bf16[32,2,16,128]{3,2,1,0:T(8,128)(2,1)S(1)}, u32[]{:S(2)}, u32[]{:S(2)}) %collective-permute-start.3) | collective-permute-done | bytes 262176 | tf_op jit(solution)/shard_map/ppermute | solution.py:221
  47.1 0.0 collective-permute-start.4
  47.1 0.0 collective-permute-done.5.refs_2_
  47.1 2.0 %shard_map.39.refs_3_ = bf16[2,512,4096]{2,1,0:T(8,128)(2,1)} custom-call(bf16[32,2,16,128]{3,2,1,0:T(8,128)(2,1)S(1)} %bitcast.8, bf16[32,2,16,128]{3,2,1,0:T(8,128)(2,1)S(1)} %collective-permute-done.refs_1_, bf16[32,2,16,128]{3,2,1,0:T(8,128)(2,1)S(1)} %collective-permute-done.5.refs_2_, ...), custom_call_target="tpu_custom_call", output_to_operand_aliasing={{}: (4, {})} | custom-call | flops 1 | bytes 1 | tf_op jit(solution)/shard_map/pallas_call | solution.py:204
  49.1 1.0 %collective-permute-done.1.refs_2_ = bf16[32,2,16,128]{3,2,1,0:T(8,128)(2,1)S(1)} collective-permute-done((bf16[32,2,16,128]{3,2,1,0:T(8,128)(2,1)S(1)}, bf16[32,2,16,128]{3,2,1,0:T(8,128)(2,1)S(1)}, u32[]{:S(2)}, u32[]{:S(2)}) %collective-permute-start.1) | collective-permute-done | bytes 262176 | tf_op jit(solution)/shard_map/ppermute | solution.py:221
  50.0 0.0 collective-permute-done.4.refs_1_
  50.0 2.4 %collective-permute-start.6 = (bf16[32,2,16,128]{3,2,1,0:T(8,128)(2,1)S(1)}, bf16[32,2,16,128]{3,2,1,0:T(8,128)(2,1)S(1)}, u32[]{:S(2)}, u32[]{:S(2)}) collective-permute-start(bf16[32,2,16,128]{3,2,1,0:T(8,128)(2,1)S(1)} %collective-permute-done.1.refs_2_), channel_id=1, source_target_pairs={{0,1},{1,0},{2,3},{3,2},{4,5},{5,4},{6,7},{7,6},{8,9},{9,8},{10,11... | collective-permute-start | bytes 786440 | tf_op jit(solution)/shard_map/ppermute | solution.py:225
  52.5 1.6 %shard_map.40.refs_2_ = bf16[2,512,4096]{2,1,0:T(8,128)(2,1)} custom-call(bf16[32,2,16,128]{3,2,1,0:T(8,128)(2,1)S(1)} %bitcast.9, bf16[32,2,16,128]{3,2,1,0:T(8,128)(2,1)S(1)} %collective-permute-done.4.refs_1_, bf16[32,2,16,128]{3,2,1,0:T(8,128)(2,1)S(1)} %collective-permute-done.1.refs_2_, ...), custom_call_target="tpu_custom_call", output_to_operand_aliasing={{}: (3, {})} | custom-call | flops 1 | bytes 1 | tf_op jit(solution)/shard_map/pallas_call | solution.py:204
  54.1 0.0 collective-permute-done.6.refs_1_
  54.1 1.2 %shard_map.41 = bf16[2,512,4096]{2,1,0:T(8,128)(2,1)} custom-call(bf16[32,2,16,128]{3,2,1,0:T(8,128)(2,1)S(1)} %bitcast.10, bf16[32,2,16,128]{3,2,1,0:T(8,128)(2,1)S(1)} %collective-permute-done.6.refs_1_, bf16[2,512,4096]{2,1,0:T(8,128)(2,1)} %shard_map.40.refs_2_), custom_call_target="tpu_custom_call", output_to_operand_aliasing={{}: (2, {})} | custom-call | flops 1 | bytes 1 | tf_op jit(solution)/shard_map/pallas_call | solution.py:204
Async XLA Ops:
  26.0 6.9 %collective-permute-start.2 = (bf16[32,2,16,128]{3,2,1,0:T(8,128)(2,1)S(1)}, bf16[32,2,16,128]{3,2,1,0:T(8,128)(2,1)S(1)}, u32[]{:S(2)}, u32[]{:S(2)}) collective-permute-start(bf16[32,2,16,128]{3,2,1,0:T(8,128)(2,1)S(1)} %bitcast.4), channel_id=1, source_target_pairs={{0,1},{1,0},{2,3},{3,2},{4,5},{5,4},{6,7},{7,6},{8,9},{9,8},{10,11... | collective-permute-start | bytes 786440 | tf_op jit(solution)/shard_map/ppermute | solution.py:225
  27.8 11.4 %collective-permute-start = (bf16[32,2,16,128]{3,2,1,0:T(8,128)(2,1)S(1)}, bf16[32,2,16,128]{3,2,1,0:T(8,128)(2,1)S(1)}, u32[]{:S(2)}, u32[]{:S(2)}) collective-permute-start(bf16[32,2,16,128]{3,2,1,0:T(8,128)(2,1)S(1)} %bitcast.5), channel_id=1, source_target_pairs={{0,2},{1,7},{2,4},{3,1},{4,6},{5,3},{6,0},{7,5},{8,10},{9,15},{10,... | collective-permute-start | bytes 786440 | tf_op jit(solution)/shard_map/ppermute | solution.py:221
  34.6 12.5 %collective-permute-start.3 = (bf16[32,2,16,128]{3,2,1,0:T(8,128)(2,1)S(1)}, bf16[32,2,16,128]{3,2,1,0:T(8,128)(2,1)S(1)}, u32[]{:S(2)}, u32[]{:S(2)}) collective-permute-start(bf16[32,2,16,128]{3,2,1,0:T(8,128)(2,1)S(1)} %collective-permute-done.2.refs_2_), channel_id=1, source_target_pairs={{0,2},{1,7},{2,4},{3,1},{4,6},{5,3},{6,0},{7,5},{8,10},{9,15},{10,... | collective-permute-start | bytes 786440 | tf_op jit(solution)/shard_map/ppermute | solution.py:221
  39.2 7.8 %collective-permute-start.5 = (bf16[32,2,16,128]{3,2,1,0:T(8,128)(2,1)S(1)}, bf16[32,2,16,128]{3,2,1,0:T(8,128)(2,1)S(1)}, u32[]{:S(2)}, u32[]{:S(2)}) collective-permute-start(bf16[32,2,16,128]{3,2,1,0:T(8,128)(2,1)S(1)} %collective-permute-done.refs_1_), channel_id=1, source_target_pairs={{0,1},{1,0},{2,3},{3,2},{4,5},{5,4},{6,7},{7,6},{8,9},{9,8},{10,11... | collective-permute-start | bytes 786440 | tf_op jit(solution)/shard_map/ppermute | solution.py:225
  40.7 9.3 %collective-permute-start.1 = (bf16[32,2,16,128]{3,2,1,0:T(8,128)(2,1)S(1)}, bf16[32,2,16,128]{3,2,1,0:T(8,128)(2,1)S(1)}, u32[]{:S(2)}, u32[]{:S(2)}) collective-permute-start(bf16[32,2,16,128]{3,2,1,0:T(8,128)(2,1)S(1)} %collective-permute-done.refs_1_), channel_id=1, source_target_pairs={{0,2},{1,7},{2,4},{3,1},{4,6},{5,3},{6,0},{7,5},{8,10},{9,15},{10,... | collective-permute-start | bytes 786440 | tf_op jit(solution)/shard_map/ppermute | solution.py:221
  47.1 3.0 %collective-permute-start.4 = (bf16[32,2,16,128]{3,2,1,0:T(8,128)(2,1)S(1)}, bf16[32,2,16,128]{3,2,1,0:T(8,128)(2,1)S(1)}, u32[]{:S(2)}, u32[]{:S(2)}) collective-permute-start(bf16[32,2,16,128]{3,2,1,0:T(8,128)(2,1)S(1)} %collective-permute-done.3.refs_3_), channel_id=1, source_target_pairs={{0,1},{1,0},{2,3},{3,2},{4,5},{5,4},{6,7},{7,6},{8,9},{9,8},{10,11... | collective-permute-start | bytes 786440 | tf_op jit(solution)/shard_map/ppermute | solution.py:225
  50.0 4.0 %collective-permute-start.6 = (bf16[32,2,16,128]{3,2,1,0:T(8,128)(2,1)S(1)}, bf16[32,2,16,128]{3,2,1,0:T(8,128)(2,1)S(1)}, u32[]{:S(2)}, u32[]{:S(2)}) collective-permute-start(bf16[32,2,16,128]{3,2,1,0:T(8,128)(2,1)S(1)} %collective-permute-done.1.refs_2_), channel_id=1, source_target_pairs={{0,1},{1,0},{2,3},{3,2},{4,5},{5,4},{6,7},{7,6},{8,9},{9,8},{10,11... | collective-permute-start | bytes 786440 | tf_op jit(solution)/shard_map/ppermute | solution.py:225
